TPU v7x, 32 devices: a whole 2x2x4 slice. The times are simulated.
32 devices in a mesh: node: 16 (over z, y, x), board: 2 (over core).
Axes of the slice: x: 2, y: 2, z: 4, core: 2. Of those that a mesh axis runs over, the one named last changes fastest.
Arguments:
- logits: float32 [2, 4, 512, 1326], P('board', None, 'node'), may hold values from -310 to 310
- pot_size: float32 [4, 512], P(None, 'node'), may hold values from 1 to 20
- node_type: int32 [4, 512], P(None, 'node'), may hold values from 0 to 2, as said below
- parent_slot: int32 [4, 512], P(None, 'node'), may hold values from 0 to 511, as said below
- range_one: float32 [2, 1326], P('board'), may hold values from 0.05 to 1
- range_two: float32 [2, 1326], P('board'), may hold values from 0.05 to 1
- hand_rank: int32 [2, 1326], P('board'), may hold values from 0 to 7461
- live_mask: int32 [2, 1326], P('board'), may hold values 0 or 1
Outputs:
- new_logits: float32 [2, 4, 512, 1326], P('board', None, 'node')
- values_half: float32 [2, 4, 512, 1326], P('board', None, 'node')
Inputs may be any that keep to these rules, and one draw needn't show every extreme that they name: `node_type`: 0 marks an inner node. At each level but the last, each aligned group of four slots holds exactly one node of type 0; the last level holds none. `parent_slot`: at level 0 every entry is 0. At a level above 0 the four nodes of an aligned group of four share one parent, a node of type 0 at the level before, and every such node is the parent of exactly one group; the parent's group index is the group's own index minus an offset of 0 to 7, one offset a level, modulo 512 / 4.
All inputs are finite; a program needn't handle non-finite values. No bound on the sum of `live_mask` on one device may be relied on, other than what follows from the above.
Results may differ from a plain program's by a relative error of at most 0.0003.
Values sent between devices are 32-bit elements; how exact they have to be, the bound alone decides.
No kernel may reach another device: no remote copies, remote signals or barrier semaphores. Data moves between devices by JAX's collectives and lax.ppermute only.
A program may use at most 64 MiB of HBM per device.

v0:
```python
import functools

import jax
import jax.numpy as jnp
import numpy as np
from jax import lax
from jax.experimental import pallas as pl
from jax.experimental.pallas import tpu as pltpu
from jax.sharding import PartitionSpec as P

LANES = 128
CARDS = 52
step_scale = 0.5
eps_value = 1e-06
MEBI = 1 << 20
CLASSES = (5, 8, 10, 16)
FAR = 5


def padded(count):
    return -(-count // LANES) * LANES


def card_rows(hand_count, wide):
    pairs = [(low, high) for low in range(CARDS) for high in range(low + 1, CARDS)]
    rows = np.full((2, wide), -1, np.int32)
    rows[:, :hand_count] = np.array(pairs[:hand_count], np.int32).T
    return rows


def payoff_kernel(hands, cards_ref, rank_ref, live_ref, out_ref, flat, left, right):
    wide = out_ref.shape[1]
    flat[...] = jnp.zeros(flat.shape, jnp.float32)
    flat[0:1, 0:hands] = rank_ref[...].astype(jnp.float32)
    flat[1:2, 0:hands] = (live_ref[...] > 0).astype(jnp.float32)
    dead = 1.0 - flat[1:2, :]
    feature = lax.broadcasted_iota(jnp.int32, (LANES, wide), 0)
    hit = (feature == cards_ref[0:1, :]) | (feature == cards_ref[1:2, :])
    base = jnp.where(hit, 1.0, 0.0)
    left[...] = jnp.where(feature == CARDS, dead, jnp.where(feature == CARDS + 1, 1.0, base))
    right[...] = jnp.where(
        feature == CARDS, 1.0, jnp.where(feature == CARDS + 1, dead, base)
    ).astype(jnp.bfloat16)
    rank_row = flat[0:1, :]
    for block in range(wide // LANES):
        part = slice(block * LANES, (block + 1) * LANES)
        left_block = left[:, part].T.astype(jnp.bfloat16)
        rank_col = jnp.broadcast_to(flat[0:1, part], (LANES, LANES)).T[:, 0:1]
        hits = jnp.dot(left_block, right[...], preferred_element_type=jnp.float32)
        compat = jnp.where(hits == 0.0, 1.0, 0.0)
        order = jnp.clip(rank_row - rank_col, -1.0, 1.0)
        out_ref[part, :] = (order * compat).astype(jnp.bfloat16)
        out_ref[wide + block * LANES : wide + (block + 1) * LANES, :] = compat.astype(jnp.bfloat16)


def payoff_blocks(hand_rank, live_mask):
    hands = hand_rank.shape[-1]
    wide = padded(hands)
    return pl.pallas_call(
        functools.partial(payoff_kernel, hands),
        out_shape=jax.ShapeDtypeStruct((2 * wide, wide), jnp.bfloat16),
        scratch_shapes=[
            pltpu.VMEM((8, wide), jnp.float32),
            pltpu.VMEM((LANES, wide), jnp.float32),
            pltpu.VMEM((LANES, wide), jnp.bfloat16),
        ],
        compiler_params=pltpu.CompilerParams(vmem_limit_bytes=20 * MEBI),
        cost_estimate=pl.CostEstimate(
            flops=2 * wide * wide * LANES, bytes_accessed=4 * wide * wide, transcendentals=0
        ),
        name="payoff",
    )(jnp.asarray(card_rows(hands, wide)), hand_rank, live_mask)


def row_count(planes, groups):
    return -(-planes * groups // 8) * 8


def plan_of(parent_ref, node_count, groups):
    total = groups * node_count
    first = lax.axis_index("node") * groups
    off = [lax.rem(first - (parent_ref[idx, 0] >> 2) + total, total) for idx in (1, 2, 3)]
    one = off[0]
    two = one + off[1]
    three = two + off[2]
    low = jnp.maximum(one, three - groups)
    high = jnp.minimum(two, groups)
    middle = jnp.minimum(jnp.maximum((one + two + three + 2) >> 2, low), high)
    return middle, middle - one, two - middle, three - middle


def class_kernel(node_count, groups, parent_ref, class_ref):
    shift = plan_of(parent_ref, node_count, groups)
    need = jnp.maximum(shift[0] + shift[1], shift[2] + shift[3])
    found = jnp.int32(0)
    for size in CLASSES[:-1]:
        found = found + (need > size).astype(jnp.int32)
    class_ref[0] = jnp.where(shift[3] > groups, len(CLASSES) - 1, found)


def size_class(parent_slot, groups):
    smem = pl.BlockSpec(memory_space=pltpu.SMEM)
    return pl.pallas_call(
        functools.partial(class_kernel, lax.axis_size("node"), groups),
        out_shape=jax.ShapeDtypeStruct((1,), jnp.int32),
        in_specs=[smem],
        out_specs=smem,
        name="size_class",
    )(parent_slot)[0]


def fill_message(stage, message_ref, size, blocks, keep_from=8):
    tiles, planes = stage.shape[:2]
    for tile in range(tiles):
        for plane in range(planes):
            for block_ref, level, start in blocks:
                stage[tile, plane, pl.ds(start, 8), :] = block_ref[level, tile, plane]
            message_ref[tile, plane * size : plane * size + size, :] = stage[
                tile, plane, keep_from : keep_from + size, :
            ]


def fill_messages(node, stage, message_refs, size, block_ref, to_left, to_right):
    even = lax.rem(node, 2) == 0
    for message_ref, on_left in zip(message_refs, (even, jnp.logical_not(even))):
        blocks = [
            (block_ref, jnp.where(on_left, near[0], far[0]), jnp.where(on_left, near[1], far[1]))
            for near, far in zip(to_left, to_right)
        ]
        fill_message(stage, message_ref, size, blocks)


def pack_kernel(node_count, size, far, parent_ref, logits_ref, pot_ref, kind_ref, *rest):
    if far:
        home_ref, odd_ref, even_ref, far_ref, raw, flat, turned, stage = rest
    else:
        home_ref, odd_ref, even_ref, raw, flat, turned, stage = rest
    levels, tiles, planes, groups, _ = home_ref.shape
    slots = 4 * groups
    hands = logits_ref.shape[-1]
    pot = pot_ref[...]
    kind = kind_ref[...]
    level = lax.broadcasted_iota(jnp.int32, pot.shape, 0)
    sign = jnp.where(level % 2 == 0, -1.0, 1.0)
    flat[...] = jnp.zeros(flat.shape, jnp.float32)
    flat[0:levels, 0:slots] = jnp.where(kind == 2, pot, 0.0)
    flat[levels : 2 * levels, 0:slots] = jnp.where(kind == 1, pot, 0.0) * sign
    turned[...] = flat[...].T
    lane = lax.broadcasted_iota(jnp.int32, (groups, LANES), 1)
    for idx in range(levels):
        raw[idx, tiles - 1] = jnp.zeros((slots, LANES), jnp.float32)
        for tile in range(tiles):
            start = tile * LANES
            stop = min(start + LANES, hands)
            raw[idx, tile, :, 0 : stop - start] = logits_ref[0, idx, :, start:stop]
            first = raw[idx, tile, pl.ds(0, groups, stride=4), :]
            for plane in range(planes):
                row = raw[idx, tile, pl.ds(plane + 1, groups, stride=4), :] - first
                if tile == tiles - 1 and plane == 0:
                    for slot in range(4):
                        scale = turned[pl.ds(slot, groups, stride=4), :]
                        row = jnp.where(lane == LANES - 8 + slot, scale[:, idx : idx + 1], row)
                        fold = scale[:, levels + idx : levels + idx + 1]
                        row = jnp.where(lane == LANES - 4 + slot, fold, row)
                home_ref[idx, tile, plane] = row
    shift = plan_of(parent_ref, node_count, groups)
    fill_messages(
        lax.axis_index("node"),
        stage,
        (odd_ref, even_ref),
        size,
        home_ref,
        [(2, 8), (3, 8 + shift[2])],
        [(1, shift[0] + shift[1]), (0, shift[0])],
    )
    if far:
        for tile in range(tiles):
            for plane in range(planes):
                far_ref[tile, plane * FAR : plane * FAR + FAR, :] = home_ref[3, tile, plane, 0:FAR, :]


def message_shapes(levels, planes, groups, wide, size, far):
    tiles = wide // LANES
    message = jax.ShapeDtypeStruct((tiles, row_count(planes, size), LANES), jnp.float32)
    shapes = [jax.ShapeDtypeStruct((levels, tiles, planes, groups, LANES), jnp.float32)]
    shapes += [message] * 2
    if far:
        shapes.append(jax.ShapeDtypeStruct((tiles, row_count(planes, FAR), LANES), jnp.float32))
    return shapes


def sent_on(odd, even, far, far_steps):
    count = lax.axis_size("node")
    edges = [(src, (src + 1) % count) for src in range(count)]
    got = []
    for message, first in ((odd, 1), (even, 0)):
        pairs = [pair for edge in edges[first::2] for pair in (edge, edge[::-1])]
        got.append(lax.ppermute(message, "node", pairs))
    for message in far:
        pairs = [(src, (src + far_steps) % count) for src in range(count)]
        got.append(lax.ppermute(message, "node", pairs))
    return got


def spread_messages(node, from_left, from_right, odd_ref, even_ref, size):
    tiles, planes = from_left.shape[:2]
    even = lax.rem(node, 2) == 0
    for tile in range(tiles):
        for plane in range(planes):
            place = slice(plane * size, plane * size + size)
            odd_part = odd_ref[tile, place, :]
            even_part = even_ref[tile, place, :]
            from_left[tile, plane, 8 : 8 + size, :] = jnp.where(even, odd_part, even_part)
            from_right[tile, plane, 8 : 8 + size, :] = jnp.where(even, even_part, odd_part)


def inner_sum(inner, rows):
    total = jnp.where(inner[0], rows[0], 0.0)
    for idx in range(1, 4):
        total = total + jnp.where(inner[idx], rows[idx], 0.0)
    return total


def softmax_four(rows):
    top = jnp.maximum(jnp.maximum(rows[0], rows[1]), jnp.maximum(rows[2], 0.0))
    lifted = [jnp.exp(-top)] + [jnp.exp(row - top) for row in rows]
    total = (lifted[0] + lifted[1]) + (lifted[2] + lifted[3])
    return [row / total for row in lifted]


def operator_q(point, show, fold, range_one, range_two, block_ref, cols, pay, top_value=None):
    wide = block_ref.shape[1]
    inner = [
        [(show[idx][slot] == 0.0) & (fold[idx][slot] == 0.0) for slot in range(4)]
        for idx in range(4)
    ]
    strategy = [softmax_four(point[idx]) for idx in range(4)]
    top_one = [range_one * row for row in strategy[0]]
    above_one = inner_sum(inner[0], top_one)
    mid_two = [range_two * row for row in strategy[1]]
    above_two = inner_sum(inner[1], mid_two)
    low_one = [above_one * row for row in strategy[2]]
    last_one = inner_sum(inner[2], low_one)
    end_two = [above_two * row for row in strategy[3]]
    wide_two = jnp.broadcast_to(range_two, above_two.shape)
    reach_rows = [
        (0, [wide_two] * 4, 1.0),
        (1, mid_two, 1.0),
        (2, [above_two] * 4, 1.0),
        (3, end_two, 1.0),
        (1, [above_one] * 4, -1.0),
        (2, low_one, -1.0),
        (3, [last_one] * 4, -1.0),
    ]
    if top_value is not None:
        reach_rows = reach_rows[1:]
    skipped = 7 - len(reach_rows)
    for unit, (idx, rows, fold_sign) in enumerate(reach_rows):
        for half in range(2):
            place = slice(unit * 32 + half * 16, unit * 32 + half * 16 + 16)
            pair = (2 * half, 2 * half + 1)
            cols[place, 0:wide] = jnp.concatenate(
                [rows[slot] * show[idx][slot] for slot in pair], axis=0
            ).astype(jnp.bfloat16)
            cols[place, wide : 2 * wide] = jnp.concatenate(
                [rows[slot] * (fold[idx][slot] * fold_sign) for slot in pair], axis=0
            ).astype(jnp.bfloat16)
    for start in range(0, wide, 2 * LANES):
        stop = min(start + 2 * LANES, wide)
        pay[:, start:stop] = jnp.dot(
            cols[...], block_ref[:, start:stop], preferred_element_type=jnp.float32
        )

    def paid(unit):
        start = (unit - skipped) * 32
        return [pay[start + slot * 8 : start + slot * 8 + 8, :] for slot in range(4)]

    def added(rows):
        return (rows[0] + rows[1]) + (rows[2] + rows[3])

    def landed(rows, kept, term):
        return [rows[slot] + jnp.where(kept[slot], term, 0.0) for slot in range(4)]

    value_two_end = paid(6)
    term_two = added([strategy[3][slot] * value_two_end[slot] for slot in range(4)])
    term_two = added(landed(paid(5), inner[2], term_two))
    value_two_mid = landed(paid(4), inner[1], term_two)
    value_one_low = landed(paid(2), inner[2], added(paid(3)))
    term_one = added([strategy[2][slot] * value_one_low[slot] for slot in range(4)])
    term_one = added(landed(paid(1), inner[1], term_one))
    if top_value is None:
        value_one_top = landed(paid(0), inner[0], term_one)
    else:
        value_one_top = [
            jnp.where(inner[0][slot], term_one, top_value[slot]) for slot in range(4)
        ]
    return [value_one_top, value_two_mid, value_one_low, value_two_end]


def squares(found):
    total = None
    for rows in found:
        for row in rows:
            total = row * row if total is None else total + row * row
    return jnp.broadcast_to(jnp.sum(total), (1, LANES))


def scale_columns(rows):
    wide = rows[0][0].shape[1]
    show = [
        [level[0][:, wide - 8 + slot : wide - 7 + slot] for slot in range(4)] for level in rows
    ]
    fold = [
        [level[0][:, wide - 4 + slot : wide - 4 + slot + 1] for slot in range(4)] for level in rows
    ]
    return show, fold


def wide_row(store, place, row_ref):
    hands = row_ref.shape[1]
    store[place : place + 1, 0:hands] = row_ref[...]
    return store[place : place + 1, :]


def first_kernel(node_count, size, far, parent_ref, home_ref, odd_ref, even_ref, *rest):
    if far:
        far_ref, rest = rest[0], rest[1:]
    one_ref, two_ref, block_ref, chain_ref, value_ref, square_ref = rest[:6]
    from_left, from_right, window, ranges, cols, pay = rest[6:]
    _, tiles, planes, groups, _ = home_ref.shape
    shift = plan_of(parent_ref, node_count, groups)
    spread_messages(lax.axis_index("node"), from_left, from_right, odd_ref, even_ref, size)
    chain = lax.broadcasted_iota(jnp.int32, (groups, LANES), 0)
    point = [[[] for _ in range(planes)] for _ in range(4)]
    for tile in range(tiles):
        for plane in range(planes):
            part = window.at[tile, plane]
            part[8:16, :] = home_ref[0, tile, plane]
            part[24:32, :] = home_ref[1, tile, plane]
            part[32:40, :] = home_ref[3, tile, plane]
            from_right[tile, plane, 0:8, :] = home_ref[2, tile, plane]
            top = jnp.where(
                chain < shift[0],
                from_left[tile, plane, 8:16, :],
                part[pl.ds(8 - shift[0], 8), :],
            )
            mid = jnp.where(
                chain < shift[1],
                from_left[tile, plane, pl.ds(8 + shift[0], 8), :],
                part[pl.ds(24 - shift[1], 8), :],
            )
            low = from_right[tile, plane, pl.ds(shift[2], 8), :]
            end = jnp.where(
                chain + shift[3] < 8,
                part[pl.ds(32 + shift[3], 8), :],
                from_right[tile, plane, pl.ds(shift[2] + shift[3], 8), :],
            )
            if far:
                part[56 : 56 + FAR, :] = far_ref[tile, plane * FAR : plane * FAR + FAR, :]
                end = jnp.where(chain + shift[3] < 16, end, part[pl.ds(40 + shift[3], 8), :])
            for idx, row in enumerate((top, mid, low, end)):
                point[idx][plane].append(row)
    point = [[jnp.concatenate(rows, axis=1) for rows in level] for level in point]
    for idx in range(4):
        for plane in range(planes):
            chain_ref[idx, plane] = point[idx][plane]
    show, fold = scale_columns(point)
    ranges[...] = jnp.zeros(ranges.shape, jnp.float32)
    range_one = wide_row(ranges, 0, one_ref)
    range_two = wide_row(ranges, 1, two_ref)
    found = operator_q(point, show, fold, range_one, range_two, block_ref, cols, pay)
    for idx in range(4):
        for slot in range(4):
            value_ref[idx, slot] = found[idx][slot]
    square_ref[...] = squares(found)


def rate_of(parts_ref, entry_count):
    square_sum = jnp.sum(parts_ref[...], axis=0, keepdims=True)[:, 0:1]
    return step_scale / jnp.sqrt(square_sum / entry_count + eps_value)


def second_kernel(node_count, entry_count, size, far, parent_ref, chain_ref, value_ref, *rest):
    parts_ref, one_ref, two_ref, block_ref, own_ref, odd_ref, even_ref = rest[:7]
    rest = rest[7:]
    if far:
        far_ref, rest = rest[0], rest[1:]
    square_ref, stage, ranges, cols, pay = rest
    _, tiles, planes, groups, _ = own_ref.shape
    rate = rate_of(parts_ref, entry_count)
    raw = [[chain_ref[idx, plane] for plane in range(3)] for idx in range(4)]
    show, fold = scale_columns(raw)
    point = [
        [
            raw[idx][plane] + rate * (value_ref[idx, plane + 1] - value_ref[idx, 0])
            for plane in range(3)
        ]
        for idx in range(4)
    ]
    ranges[...] = jnp.zeros(ranges.shape, jnp.float32)
    range_one = wide_row(ranges, 0, one_ref)
    range_two = wide_row(ranges, 1, two_ref)
    top_value = [value_ref[0, slot] for slot in range(4)]
    found = operator_q(point, show, fold, range_one, range_two, block_ref, cols, pay, top_value)
    square_ref[...] = squares(found)
    for idx in range(4):
        for slot in range(4):
            for tile in range(tiles):
                own_ref[idx, tile, slot] = found[idx][slot][:, tile * LANES : (tile + 1) * LANES]
    shift = plan_of(parent_ref, node_count, groups)
    fill_messages(
        lax.axis_index("node"),
        stage,
        (odd_ref, even_ref),
        size,
        own_ref,
        [(0, 8), (1, 8 + shift[0])],
        [(3, shift[2] + shift[3]), (2, shift[2])],
    )
    if far:
        for tile in range(tiles):
            for plane in range(planes):
                stage[tile, plane, pl.ds(jnp.maximum(shift[3] - 8, 0), 8), :] = own_ref[
                    3, tile, plane
                ]
                far_ref[tile, plane * FAR : plane * FAR + FAR, :] = stage[tile, plane, 8 : 8 + FAR, :]


def last_kernel(node_count, entry_count, size, far, parent_ref, own_ref, odd_ref, even_ref, *rest):
    if far:
        far_ref, rest = rest[0], rest[1:]
    parts_ref, logits_ref, new_ref, half_ref, from_left, from_right, window, lined = rest
    _, tiles, planes, groups, _ = own_ref.shape
    hands = logits_ref.shape[-1]
    shift = plan_of(parent_ref, node_count, groups)
    rate = rate_of(parts_ref, entry_count)
    spread_messages(lax.axis_index("node"), from_left, from_right, odd_ref, even_ref, size)
    group = lax.broadcasted_iota(jnp.int32, (groups, LANES), 0)
    for tile in range(tiles):
        start = tile * LANES
        stop = min(start + LANES, hands)
        for plane in range(planes):
            part = window.at[tile, plane]
            part[0:8, :] = own_ref[1, tile, plane]
            part[24:32, :] = own_ref[2, tile, plane]
            part[40:48, :] = own_ref[3, tile, plane]
            from_right[tile, plane, 0:8, :] = own_ref[0, tile, plane]
            top = from_right[tile, plane, pl.ds(shift[0], 8), :]
            mid = jnp.where(
                group + shift[1] < 8,
                part[pl.ds(shift[1], 8), :],
                from_right[tile, plane, pl.ds(shift[0] + shift[1], 8), :],
            )
            low = jnp.where(
                group < shift[2],
                from_left[tile, plane, 8:16, :],
                part[pl.ds(24 - shift[2], 8), :],
            )
            end = jnp.where(
                group < shift[3],
                from_left[tile, plane, pl.ds(8 + shift[2], 8), :],
                part[pl.ds(40 - jnp.minimum(shift[3], 8), 8), :],
            )
            if far:
                part[56 : 56 + FAR, :] = far_ref[tile, plane * FAR : plane * FAR + FAR, :]
                end = jnp.where(group < shift[3] - 8, part[56:64, :], end)
            for idx, row in enumerate((top, mid, low, end)):
                lined[idx, tile, pl.ds(plane, groups, stride=4), :] = row
        for idx in range(4):
            value = lined[idx, tile][:, 0 : stop - start]
            half_ref[0, idx, :, start:stop] = value
            new_ref[0, idx, :, start:stop] = logits_ref[0, idx, :, start:stop] + rate * value


def shared_parts(part):
    count = lax.axis_size("node") * lax.axis_size("board")
    spread = jnp.broadcast_to(part, (count, LANES))
    return lax.all_to_all(spread, ("node", "board"), 0, 0, tiled=True)


def step_of_class(
    size,
    far,
    logits,
    pot_size,
    node_type,
    parent_slot,
    range_one,
    range_two,
    hand_rank,
    live_mask,
):
    _, levels, slots, hands = logits.shape
    wide = padded(hands)
    tiles = wide // LANES
    groups = slots // 4
    node_count = lax.axis_size("node")
    entry_count = float(logits.size * node_count * lax.axis_size("board"))
    vmem = pl.BlockSpec(memory_space=pltpu.VMEM)
    smem = pl.BlockSpec(memory_space=pltpu.SMEM)
    f32 = jnp.float32

    def limit(mebi):
        return pltpu.CompilerParams(vmem_limit_bytes=mebi * MEBI)

    def stage(planes, rows=32):
        return pltpu.VMEM((tiles, planes, rows, LANES), f32)

    home, *sent = pl.pallas_call(
        functools.partial(pack_kernel, node_count, size, far),
        out_shape=message_shapes(levels, 3, groups, wide, size, far),
        in_specs=[smem] + [vmem] * 3,
        scratch_shapes=[
            pltpu.VMEM((levels, tiles, slots, LANES), f32),
            pltpu.VMEM((LANES, LANES), f32),
            pltpu.VMEM((LANES, LANES), f32),
            stage(3),
        ],
        compiler_params=limit(12),
        name="pack",
    )(parent_slot, logits, pot_size, node_type)
    got = sent_on(sent[0], sent[1], sent[2:], -2)
    blocks = payoff_blocks(hand_rank, live_mask)
    rows = 7 * slots

    def work(count):
        return [
            pltpu.VMEM((8, wide), f32),
            pltpu.VMEM((count, 2 * wide), jnp.bfloat16),
            pltpu.VMEM((count, wide), f32),
        ]

    def cost(count):
        return pl.CostEstimate(
            flops=4 * count * wide * wide, bytes_accessed=6 * wide * wide, transcendentals=0
        )

    square_shape = jax.ShapeDtypeStruct((1, LANES), f32)
    chain, value, part = pl.pallas_call(
        functools.partial(first_kernel, node_count, size, far),
        out_shape=(
            jax.ShapeDtypeStruct((levels, 3, groups, wide), f32),
            jax.ShapeDtypeStruct((levels, 4, groups, wide), f32),
            square_shape,
        ),
        in_specs=[smem] + [vmem] * (4 + len(got)),
        scratch_shapes=[stage(3), stage(3), stage(3, 64)] + work(rows),
        compiler_params=limit(32),
        cost_estimate=cost(rows),
        name="first",
    )(parent_slot, home, *got, range_one, range_two, blocks)
    parts = shared_parts(part)
    own, *sent, part = pl.pallas_call(
        functools.partial(second_kernel, node_count, entry_count, size, far),
        out_shape=message_shapes(levels, 4, groups, wide, size, far) + [square_shape],
        in_specs=[smem] + [vmem] * 6,
        scratch_shapes=[stage(4)] + work(rows - slots),
        compiler_params=limit(32),
        cost_estimate=cost(rows - slots),
        name="second",
    )(parent_slot, chain, value, parts, range_one, range_two, blocks)
    got = sent_on(sent[0], sent[1], sent[2:], 2)
    parts = shared_parts(part)
    out_shape = jax.ShapeDtypeStruct(logits.shape, f32)
    return pl.pallas_call(
        functools.partial(last_kernel, node_count, entry_count, size, far),
        out_shape=(out_shape, out_shape),
        in_specs=[smem] + [vmem] * (3 + len(got)),
        scratch_shapes=[
            stage(4),
            stage(4),
            stage(4, 64),
            pltpu.VMEM((levels, tiles, slots, LANES), f32),
        ],
        compiler_params=limit(24),
        name="last",
    )(parent_slot, own, *got, parts, logits)


def per_device(
    logits, pot_size, node_type, parent_slot, range_one, range_two, hand_rank, live_mask
):
    branches = [
        functools.partial(step_of_class, size, size == CLASSES[-1]) for size in CLASSES
    ]
    return lax.switch(
        size_class(parent_slot, logits.shape[2] // 4),
        branches,
        logits,
        pot_size,
        node_type,
        parent_slot,
        range_one,
        range_two,
        hand_rank,
        live_mask,
    )


def solution(mesh):
    return jax.shard_map(
        per_device,
        mesh=mesh,
        in_specs=(
            P("board", None, "node", None),
            P(None, "node"),
            P(None, "node"),
            P(None, "node"),
            P("board", None),
            P("board", None),
            P("board", None),
            P("board", None),
        ),
        out_specs=(P("board", None, "node", None), P("board", None, "node", None)),
        check_vma=False,
    )
```

profile of v0, /device:TPU:0, one launch (start us, length us, event | category | flops | bytes accessed | tf_op | source)
XLA Modules:
  0.0 51.9 jit_solution(3154034410401642321)
XLA Ops:
  0.6 1.2 %size_class.1 = s32[1]{0:T(128)} custom-call(s32[4,32]{1,0:T(4,128)} %parent_ref.1), custom_call_target="tpu_custom_call" | custom-call | tf_op jit(solution)/shard_map/size_class/pallas_call | solution.py:103
  2.5 49.4 %conditional.1 = ((f32[1,4,32,1326]{3,2,1,0:T(8,128)}, f32[1,4,32,1326]{3,2,1,0:T(8,128)})) conditional(s32[]{:T(128)} %bitcast.16, (s32[4,32]{1,0:T(4,128)}, f32[1,4,32,1326]{3,2,1,0:T(8,128)}, f32[4,32]{1,0:T(4,128)}, s32[4,32]{1,0:T(4,128)}, s32[2,1408]{1,0:T(2,128)}, /*index=5*/s32[1,1326]{1,0:T(1,128)}, ...), branch_computations={%region_0.0_spmd, %region_1.0_spmd, %region_2.0_spmd, %region_3.0_... | conditional | flops 3806330880 | bytes 40526632 | solution.py:586
  2.8 0.0 copy-start.6
  2.8 0.0 copy-start.10
  2.8 0.0 copy-start.14
  2.8 1.7 %pack.6 = (f32[4,11,3,8,128]{4,3,2,1,0:T(8,128)S(1)}, f32[11,32,128]{2,1,0:T(8,128)S(1)}, f32[11,32,128]{2,1,0:T(8,128)S(1)}) custom-call(s32[4,32]{1,0:T(4,128)} %get-tuple-element.110.parent_ref, f32[1,4,32,1326]{3,2,1,0:T(8,128)} %get-tuple-element.111.logits_ref.rest_1_, f32[4,32]{1,0:T(4,128)} %get-tuple-element.112.pot_ref, ...), custom_call_target="tpu_custom_call" | custom-call | tf_op jit(solution)/shard_map/cond/branch_2_fun/pack/pallas_call | solution.py:509
  4.5 7.0 %collective-permute-start.8 = (f32[11,32,128]{2,1,0:T(8,128)S(1)}, f32[11,32,128]{2,1,0:T(8,128)S(1)}, u32[]{:S(2)}, u32[]{:S(2)}) collective-permute-start(f32[11,32,128]{2,1,0:T(8,128)S(1)} %get-tuple-element.115), channel_id=1, source_target_pairs={{2,4},{4,2},{6,8},{8,6},{10,12},{12,10},{14,16},{16,14},{18,20},{2... | collective-permute-start | bytes 540680 | tf_op jit(solution)/shard_map/cond/branch_2_fun/ppermute | solution.py:198
  11.5 0.0 collective-permute-start.9
  11.5 2.8 %payoff.6.rest_2_.rest_3_ = bf16[2816,1408]{1,0:T(8,128)(2,1)S(1)} custom-call(s32[2,1408]{1,0:T(2,128)} %get-tuple-element.119.cards_ref, s32[1,1326]{1,0:T(1,128)} %get-tuple-element.120.rank_ref, s32[1,1326]{1,0:T(1,128)} %get-tuple-element.121.live_ref), custom_call_target="tpu_custom_call" | custom-call | flops 507510784 | bytes 7929856 | tf_op jit(solution)/shard_map/cond/branch_2_fun/payoff/pallas_call | solution.py:59
  14.3 1.8 %collective-permute-done.8.odd_ref = f32[11,32,128]{2,1,0:T(8,128)S(1)} collective-permute-done((f32[11,32,128]{2,1,0:T(8,128)S(1)}, f32[11,32,128]{2,1,0:T(8,128)S(1)}, u32[]{:S(2)}, u32[]{:S(2)}) %collective-permute-start.8) | collective-permute-done | bytes 180256 | tf_op jit(solution)/shard_map/cond/branch_2_fun/ppermute | solution.py:198
  16.1 1.4 %collective-permute-done.9.even_ref = f32[11,32,128]{2,1,0:T(8,128)S(1)} collective-permute-done((f32[11,32,128]{2,1,0:T(8,128)S(1)}, f32[11,32,128]{2,1,0:T(8,128)S(1)}, u32[]{:S(2)}, u32[]{:S(2)}) %collective-permute-start.9) | collective-permute-done | bytes 180256 | tf_op jit(solution)/shard_map/cond/branch_2_fun/ppermute | solution.py:198
  17.5 0.0 copy-done.6
  17.5 0.0 copy-done.10
  17.5 0.0 copy-done.14
  17.5 0.0 copy-start.2
  17.5 3.5 %first.6 = (f32[4,3,8,1408]{3,2,1,0:T(8,128)S(1)}, f32[4,4,8,1408]{3,2,1,0:T(8,128)S(1)}, f32[1,128]{1,0:T(1,128)S(1)}) custom-call(s32[4,32]{1,0:T(4,128)S(1)} %copy-done.6, f32[4,11,3,8,128]{4,3,2,1,0:T(8,128)S(1)} %get-tuple-element.114.home_ref, f32[11,32,128]{2,1,0:T(8,128)S(1)} %collective-permute-done.8.odd_ref, ...), custom_call_target="tpu_custom_call" | custom-call | flops 1776287744 | bytes 11894784 | tf_op jit(solution)/shard_map/cond/branch_2_fun/first/pallas_call | solution.py:539
  21.1 11.7 %all_to_all.52 = f32[32,1,128]{2,1,0:T(1,128)S(1)} all-to-all(f32[32,1,128]{2,1,0:T(1,128)S(1)} %broadcast_in_dim.24), channel_id=1, replica_groups=mesh['node'=16,'board'=2] {'node','board'}, dimensions={0} | all-to-all | bytes 32768 | tf_op jit(solution)/shard_map/cond/branch_2_fun/all_to_all | solution.py:478
  32.8 3.4 %second.6 = (f32[4,11,4,8,128]{4,3,2,1,0:T(8,128)S(1)}, f32[11,40,128]{2,1,0:T(8,128)S(1)}, f32[11,40,128]{2,1,0:T(8,128)S(1)}, f32[1,128]{1,0:T(1,128)S(1)}) custom-call(s32[4,32]{1,0:T(4,128)S(1)} %copy-done.6, f32[4,3,8,1408]{3,2,1,0:T(8,128)S(1)} %get-tuple-element.122.chain_ref, f32[4,4,8,1408]{3,2,1,0:T(8,128)S(1)} %get-tuple-element.123.value_ref, ...), custom_call_target="tpu_custom_call" | custom-call | flops 1522532352 | bytes 11894784 | tf_op jit(solution)/shard_map/cond/branch_2_fun/second/pallas_call | solution.py:553
  36.2 0.6 %collective-permute-start.10 = (f32[11,40,128]{2,1,0:T(8,128)S(1)}, f32[11,40,128]{2,1,0:T(8,128)S(1)}, u32[]{:S(2)}, u32[]{:S(2)}) collective-permute-start(f32[11,40,128]{2,1,0:T(8,128)S(1)} %get-tuple-element.126), channel_id=1, source_target_pairs={{2,4},{4,2},{6,8},{8,6},{10,12},{12,10},{14,16},{16,14},{18,20},{2... | collective-permute-start | bytes 675848 | tf_op jit(solution)/shard_map/cond/branch_2_fun/ppermute | solution.py:198
  36.8 1.4 %collective-permute-start.11 = (f32[11,40,128]{2,1,0:T(8,128)S(1)}, f32[11,40,128]{2,1,0:T(8,128)S(1)}, u32[]{:S(2)}, u32[]{:S(2)}) collective-permute-start(f32[11,40,128]{2,1,0:T(8,128)S(1)} %get-tuple-element.127), channel_id=1, source_target_pairs={{0,2},{2,0},{4,6},{6,4},{8,10},{10,8},{12,14},{14,12},{16,18},{18,... | collective-permute-start | bytes 675848 | tf_op jit(solution)/shard_map/cond/branch_2_fun/ppermute | solution.py:198
  38.3 11.5 %all_to_all.53 = f32[32,1,128]{2,1,0:T(1,128)S(1)} all-to-all(f32[32,1,128]{2,1,0:T(1,128)S(1)} %broadcast_in_dim.25), channel_id=1, replica_groups=mesh['node'=16,'board'=2] {'node','board'}, dimensions={0} | all-to-all | bytes 32768 | tf_op jit(solution)/shard_map/cond/branch_2_fun/all_to_all | solution.py:478
  49.8 0.0 collective-permute-done.10.odd_ref
  49.8 0.0 collective-permute-done.11.even_ref
  49.8 0.0 copy-done.2
  49.8 2.1 %last.6 = (f32[1,4,32,1326]{3,2,1,0:T(8,128)}, f32[1,4,32,1326]{3,2,1,0:T(8,128)}) custom-call(s32[4,32]{1,0:T(4,128)S(1)} %copy-done.6, f32[4,11,4,8,128]{4,3,2,1,0:T(8,128)S(1)} %get-tuple-element.125.own_ref, f32[11,40,128]{2,1,0:T(8,128)S(1)} %collective-permute-done.10.odd_ref, f32[11,40,128]{2,1,0:T(8,128)S(1)} %collective-permute-done.11.even_ref, ...), custom_call_target="tpu_custom_call" | custom-call | tf_op jit(solution)/shard_map/cond/branch_2_fun/last/pallas_call | solution.py:565
  (2 shorter events, 0.0 us)
Async XLA Ops:
  2.8 14.7 %copy-start.6 = (s32[4,32]{1,0:T(4,128)S(1)}, s32[4,32]{1,0:T(4,128)}, u32[]{:S(2)}) copy-start(s32[4,32]{1,0:T(4,128)} %get-tuple-element.110.parent_ref) | copy-start | bytes 1540 | tf_op jit(solution)/shard_map/cond
  2.8 14.7 %copy-start.10 = (f32[1,1326]{1,0:T(1,128)S(1)}, f32[1,1326]{1,0:T(1,128)}, u32[]{:S(2)}) copy-start(f32[1,1326]{1,0:T(1,128)} %get-tuple-element.117.rest_0_.rest_1_) | copy-start | bytes 15916 | tf_op jit(solution)/shard_map/cond
  2.8 14.7 %copy-start.14 = (f32[1,1326]{1,0:T(1,128)S(1)}, f32[1,1326]{1,0:T(1,128)}, u32[]{:S(2)}) copy-start(f32[1,1326]{1,0:T(1,128)} %get-tuple-element.118.rest_1_.rest_2_) | copy-start | bytes 15916 | tf_op jit(solution)/shard_map/cond
  4.5 11.6 %collective-permute-start.8 = (f32[11,32,128]{2,1,0:T(8,128)S(1)}, f32[11,32,128]{2,1,0:T(8,128)S(1)}, u32[]{:S(2)}, u32[]{:S(2)}) collective-permute-start(f32[11,32,128]{2,1,0:T(8,128)S(1)} %get-tuple-element.115), channel_id=1, source_target_pairs={{2,4},{4,2},{6,8},{8,6},{10,12},{12,10},{14,16},{16,14},{18,20},{2... | collective-permute-start | bytes 540680 | tf_op jit(solution)/shard_map/cond/branch_2_fun/ppermute | solution.py:198
  11.5 6.0 %collective-permute-start.9 = (f32[11,32,128]{2,1,0:T(8,128)S(1)}, f32[11,32,128]{2,1,0:T(8,128)S(1)}, u32[]{:S(2)}, u32[]{:S(2)}) collective-permute-start(f32[11,32,128]{2,1,0:T(8,128)S(1)} %get-tuple-element.116), channel_id=1, source_target_pairs={{0,2},{2,0},{4,6},{6,4},{8,10},{10,8},{12,14},{14,12},{16,18},{18,... | collective-permute-start | bytes 540680 | tf_op jit(solution)/shard_map/cond/branch_2_fun/ppermute | solution.py:198
  17.5 32.3 %copy-start.2 = (f32[1,4,32,1326]{3,2,1,0:T(8,128)S(1)}, f32[1,4,32,1326]{3,2,1,0:T(8,128)}, u32[]{:S(2)}) copy-start(f32[1,4,32,1326]{3,2,1,0:T(8,128)} %get-tuple-element.111.logits_ref.rest_1_) | copy-start | bytes 2036740 | tf_op jit(solution)/shard_map/cond
  36.2 13.6 %collective-permute-start.10 = (f32[11,40,128]{2,1,0:T(8,128)S(1)}, f32[11,40,128]{2,1,0:T(8,128)S(1)}, u32[]{:S(2)}, u32[]{:S(2)}) collective-permute-start(f32[11,40,128]{2,1,0:T(8,128)S(1)} %get-tuple-element.126), channel_id=1, source_target_pairs={{2,4},{4,2},{6,8},{8,6},{10,12},{12,10},{14,16},{16,14},{18,20},{2... | collective-permute-start | bytes 675848 | tf_op jit(solution)/shard_map/cond/branch_2_fun/ppermute | solution.py:198
  36.8 13.0 %collective-permute-start.11 = (f32[11,40,128]{2,1,0:T(8,128)S(1)}, f32[11,40,128]{2,1,0:T(8,128)S(1)}, u32[]{:S(2)}, u32[]{:S(2)}) collective-permute-start(f32[11,40,128]{2,1,0:T(8,128)S(1)} %get-tuple-element.127), channel_id=1, source_target_pairs={{0,2},{2,0},{4,6},{6,4},{8,10},{10,8},{12,14},{14,12},{16,18},{18,... | collective-permute-start | bytes 675848 | tf_op jit(solution)/shard_map/cond/branch_2_fun/ppermute | solution.py:198
where the time goes:
time: 52.2 us; the launch traced here: 51.9 us
  blocking collectives  23.2 us (44%)
  Pallas kernels  14.8 us (28%)
  starting transfers between devices  9.07 us (17%)
  waiting for transfers between devices  3.16 us (6%)
  between operations  1.29 us (2%)
    all_to_all x2, blocking collectives, shared_parts(): return lax.all_to_all(spread, ('node', 'board'), 0, 0, tiled=True)  23.2 us
    ppermute x4, starting transfers between devices, sent_on(): got.append(lax.ppermute(message, 'node', pairs))  9.07 us
    pallas_call x1, Pallas kernels, step_of_class(): pl.pallas_call(functools.partial(first_kernel, node_count, size, far), ou...  3.51 us
    pallas_call x1, Pallas kernels, step_of_class(): pl.pallas_call(functools.partial(second_kernel, node_count, entry_count,...  3.41 us
    ppermute x4, waiting for transfers between devices, sent_on(): got.append(lax.ppermute(message, 'node', pairs))  3.16 us
    pallas_call x1, Pallas kernels, payoff_blocks(): pl.pallas_call(functools.partial(payoff_kernel, hands), out_shape=jax.Sha...  2.84 us
    pallas_call x1, Pallas kernels, step_of_class(): pl.pallas_call(functools.partial(last_kernel, node_count, entry_count, si...  2.14 us
    pallas_call x1, Pallas kernels, step_of_class(): pl.pallas_call(functools.partial(pack_kernel, node_count, size, far), out...  1.69 us
  transfers between devices with their start and end apart: 4, of which 2 were waited for; matrix products, arithmetic and copies ran while one was open for 0% of the time, Pallas kernels for 5%

commit v1 on v0

--- a/solution.py
+++ b/solution.py
@@ -89,64 +89,46 @@
     return middle, middle - one, two - middle, three - middle
 
 
-def class_kernel(node_count, groups, parent_ref, class_ref):
-    shift = plan_of(parent_ref, node_count, groups)
+def class_of(shift, groups):
     need = jnp.maximum(shift[0] + shift[1], shift[2] + shift[3])
     found = jnp.int32(0)
     for size in CLASSES[:-1]:
         found = found + (need > size).astype(jnp.int32)
-    class_ref[0] = jnp.where(shift[3] > groups, len(CLASSES) - 1, found)
-
-
-def size_class(parent_slot, groups):
-    smem = pl.BlockSpec(memory_space=pltpu.SMEM)
-    return pl.pallas_call(
-        functools.partial(class_kernel, lax.axis_size("node"), groups),
-        out_shape=jax.ShapeDtypeStruct((1,), jnp.int32),
-        in_specs=[smem],
-        out_specs=smem,
-        name="size_class",
-    )(parent_slot)[0]
-
-
-def fill_message(stage, message_ref, size, blocks, keep_from=8):
+    return jnp.where(shift[3] > groups, len(CLASSES) - 1, found)
+
+
+def fill_message(stage, message_ref, size, blocks, tail_ref):
     tiles, planes = stage.shape[:2]
     for tile in range(tiles):
         for plane in range(planes):
             for block_ref, level, start in blocks:
-                stage[tile, plane, pl.ds(start, 8), :] = block_ref[level, tile, plane]
+                if tail_ref is not None and tile == tiles - 1 and plane == 0:
+                    block = tail_ref[level]
+                else:
+                    block = block_ref[level, tile, plane]
+                stage[tile, plane, pl.ds(start, 8), :] = block
             message_ref[tile, plane * size : plane * size + size, :] = stage[
-                tile, plane, keep_from : keep_from + size, :
+                tile, plane, 8 : 8 + size, :
             ]
 
 
-def fill_messages(node, stage, message_refs, size, block_ref, to_left, to_right):
+def fill_messages(
+    node, stage, message_refs, size, block_ref, to_left, to_right, tail_ref=None
+):
     even = lax.rem(node, 2) == 0
     for message_ref, on_left in zip(message_refs, (even, jnp.logical_not(even))):
         blocks = [
             (block_ref, jnp.where(on_left, near[0], far[0]), jnp.where(on_left, near[1], far[1]))
             for near, far in zip(to_left, to_right)
         ]
-        fill_message(stage, message_ref, size, blocks)
-
-
-def pack_kernel(node_count, size, far, parent_ref, logits_ref, pot_ref, kind_ref, *rest):
-    if far:
-        home_ref, odd_ref, even_ref, far_ref, raw, flat, turned, stage = rest
-    else:
-        home_ref, odd_ref, even_ref, raw, flat, turned, stage = rest
+        fill_message(stage, message_ref, size, blocks, tail_ref)
+
+
+def prepare_kernel(node_count, parent_ref, logits_ref, home_ref, class_ref, raw):
     levels, tiles, planes, groups, _ = home_ref.shape
     slots = 4 * groups
     hands = logits_ref.shape[-1]
-    pot = pot_ref[...]
-    kind = kind_ref[...]
-    level = lax.broadcasted_iota(jnp.int32, pot.shape, 0)
-    sign = jnp.where(level % 2 == 0, -1.0, 1.0)
-    flat[...] = jnp.zeros(flat.shape, jnp.float32)
-    flat[0:levels, 0:slots] = jnp.where(kind == 2, pot, 0.0)
-    flat[levels : 2 * levels, 0:slots] = jnp.where(kind == 1, pot, 0.0) * sign
-    turned[...] = flat[...].T
-    lane = lax.broadcasted_iota(jnp.int32, (groups, LANES), 1)
+    class_ref[0] = class_of(plan_of(parent_ref, node_count, groups), groups)
     for idx in range(levels):
         raw[idx, tiles - 1] = jnp.zeros((slots, LANES), jnp.float32)
         for tile in range(tiles):
@@ -156,13 +138,61 @@
             first = raw[idx, tile, pl.ds(0, groups, stride=4), :]
             for plane in range(planes):
                 row = raw[idx, tile, pl.ds(plane + 1, groups, stride=4), :] - first
-                if tile == tiles - 1 and plane == 0:
-                    for slot in range(4):
-                        scale = turned[pl.ds(slot, groups, stride=4), :]
-                        row = jnp.where(lane == LANES - 8 + slot, scale[:, idx : idx + 1], row)
-                        fold = scale[:, levels + idx : levels + idx + 1]
-                        row = jnp.where(lane == LANES - 4 + slot, fold, row)
                 home_ref[idx, tile, plane] = row
+
+
+def prepared(logits, parent_slot):
+    _, levels, slots, hands = logits.shape
+    groups = slots // 4
+    tiles = padded(hands) // LANES
+    vmem = pl.BlockSpec(memory_space=pltpu.VMEM)
+    smem = pl.BlockSpec(memory_space=pltpu.SMEM)
+    return pl.pallas_call(
+        functools.partial(prepare_kernel, lax.axis_size("node")),
+        out_shape=(
+            jax.ShapeDtypeStruct((levels, tiles, 3, groups, LANES), jnp.float32),
+            jax.ShapeDtypeStruct((1,), jnp.int32),
+        ),
+        in_specs=[smem, vmem],
+        out_specs=(vmem, smem),
+        scratch_shapes=[pltpu.VMEM((levels, tiles, slots, LANES), jnp.float32)],
+        compiler_params=pltpu.CompilerParams(vmem_limit_bytes=10 * MEBI),
+        name="prepare",
+    )(parent_slot, logits)
+
+
+def pack_kernel(
+    node_count,
+    size,
+    far,
+    parent_ref,
+    pot_ref,
+    kind_ref,
+    home_ref,
+    odd_ref,
+    even_ref,
+    *rest,
+):
+    far_ref = rest[0] if far else None
+    tail_ref, stage = rest[-2:]
+    levels, tiles, planes, groups, _ = home_ref.shape
+    group = lax.broadcasted_iota(jnp.int32, (groups, LANES), 0)
+    lane = lax.broadcasted_iota(jnp.int32, (groups, LANES), 1)
+    spot = [
+        [(group == row) & (lane == LANES - 8 + column) for column in range(8)]
+        for row in range(groups)
+    ]
+    for idx in range(levels):
+        sign = -1.0 if idx % 2 == 0 else 1.0
+        row = home_ref[idx, tiles - 1, 0]
+        for place in range(4 * groups):
+            pot = pot_ref[idx, place]
+            kind = kind_ref[idx, place]
+            show = jnp.where(kind == 2, pot, 0.0)
+            fold = jnp.where(kind == 1, pot, 0.0) * sign
+            row = jnp.where(spot[place // 4][place % 4], show, row)
+            row = jnp.where(spot[place // 4][place % 4 + 4], fold, row)
+        tail_ref[idx] = row
     shift = plan_of(parent_ref, node_count, groups)
     fill_messages(
         lax.axis_index("node"),
@@ -172,18 +202,21 @@
         home_ref,
         [(2, 8), (3, 8 + shift[2])],
         [(1, shift[0] + shift[1]), (0, shift[0])],
+        tail_ref,
     )
     if far:
         for tile in range(tiles):
             for plane in range(planes):
-                far_ref[tile, plane * FAR : plane * FAR + FAR, :] = home_ref[3, tile, plane, 0:FAR, :]
-
-
-def message_shapes(levels, planes, groups, wide, size, far):
+                block = home_ref[3, tile, plane]
+                if tile == tiles - 1 and plane == 0:
+                    block = tail_ref[3]
+                far_ref[tile, plane * FAR : plane * FAR + FAR, :] = block[0:FAR, :]
+
+
+def message_shapes(planes, wide, size, far):
     tiles = wide // LANES
     message = jax.ShapeDtypeStruct((tiles, row_count(planes, size), LANES), jnp.float32)
-    shapes = [jax.ShapeDtypeStruct((levels, tiles, planes, groups, LANES), jnp.float32)]
-    shapes += [message] * 2
+    shapes = [message] * 2
     if far:
         shapes.append(jax.ShapeDtypeStruct((tiles, row_count(planes, FAR), LANES), jnp.float32))
     return shapes
@@ -228,7 +261,7 @@
     return [row / total for row in lifted]
 
 
-def operator_q(point, show, fold, range_one, range_two, block_ref, cols, pay, top_value=None):
+def operator_q(point, show, fold, range_one, range_two, block_ref, cols, put, top_ref=None):
     wide = block_ref.shape[1]
     inner = [
         [(show[idx][slot] == 0.0) & (fold[idx][slot] == 0.0) for slot in range(4)]
@@ -252,7 +285,7 @@
         (2, low_one, -1.0),
         (3, [last_one] * 4, -1.0),
     ]
-    if top_value is not None:
+    if top_ref is not None:
         reach_rows = reach_rows[1:]
     skipped = 7 - len(reach_rows)
     for unit, (idx, rows, fold_sign) in enumerate(reach_rows):
@@ -265,36 +298,41 @@
             cols[place, wide : 2 * wide] = jnp.concatenate(
                 [rows[slot] * (fold[idx][slot] * fold_sign) for slot in pair], axis=0
             ).astype(jnp.bfloat16)
+    def added(rows):
+        return (rows[0] + rows[1]) + (rows[2] + rows[3])
+
+    def landed(rows, kept, term):
+        return [rows[slot] + jnp.where(kept[slot], term, 0.0) for slot in range(4)]
+
+    total = None
     for start in range(0, wide, 2 * LANES):
         stop = min(start + 2 * LANES, wide)
-        pay[:, start:stop] = jnp.dot(
-            cols[...], block_ref[:, start:stop], preferred_element_type=jnp.float32
-        )
-
-    def paid(unit):
-        start = (unit - skipped) * 32
-        return [pay[start + slot * 8 : start + slot * 8 + 8, :] for slot in range(4)]
-
-    def added(rows):
-        return (rows[0] + rows[1]) + (rows[2] + rows[3])
-
-    def landed(rows, kept, term):
-        return [rows[slot] + jnp.where(kept[slot], term, 0.0) for slot in range(4)]
-
-    value_two_end = paid(6)
-    term_two = added([strategy[3][slot] * value_two_end[slot] for slot in range(4)])
-    term_two = added(landed(paid(5), inner[2], term_two))
-    value_two_mid = landed(paid(4), inner[1], term_two)
-    value_one_low = landed(paid(2), inner[2], added(paid(3)))
-    term_one = added([strategy[2][slot] * value_one_low[slot] for slot in range(4)])
-    term_one = added(landed(paid(1), inner[1], term_one))
-    if top_value is None:
-        value_one_top = landed(paid(0), inner[0], term_one)
-    else:
-        value_one_top = [
-            jnp.where(inner[0][slot], term_one, top_value[slot]) for slot in range(4)
-        ]
-    return [value_one_top, value_two_mid, value_one_low, value_two_end]
+        pay = jnp.dot(cols[...], block_ref[:, start:stop], preferred_element_type=jnp.float32)
+
+        def paid(unit):
+            first = (unit - skipped) * 32
+            return [pay[first + slot * 8 : first + slot * 8 + 8, :] for slot in range(4)]
+
+        def weighed(idx, rows):
+            return added([strategy[idx][slot][:, start:stop] * rows[slot] for slot in range(4)])
+
+        value_two_end = paid(6)
+        term_two = added(landed(paid(5), inner[2], weighed(3, value_two_end)))
+        value_two_mid = landed(paid(4), inner[1], term_two)
+        value_one_low = landed(paid(2), inner[2], added(paid(3)))
+        term_one = added(landed(paid(1), inner[1], weighed(2, value_one_low)))
+        if top_ref is None:
+            value_one_top = landed(paid(0), inner[0], term_one)
+        else:
+            value_one_top = [
+                jnp.where(inner[0][slot], term_one, top_ref[0, slot, :, start:stop])
+                for slot in range(4)
+            ]
+        found = [value_one_top, value_two_mid, value_one_low, value_two_end]
+        put(start, stop, found)
+        part = squares(found)
+        total = part if total is None else total + part
+    return total
 
 
 def squares(found):
@@ -322,11 +360,11 @@
     return store[place : place + 1, :]
 
 
-def first_kernel(node_count, size, far, parent_ref, home_ref, odd_ref, even_ref, *rest):
+def first_kernel(node_count, size, far, parent_ref, home_ref, tail_ref, odd_ref, even_ref, *rest):
     if far:
         far_ref, rest = rest[0], rest[1:]
     one_ref, two_ref, block_ref, chain_ref, value_ref, square_ref = rest[:6]
-    from_left, from_right, window, ranges, cols, pay = rest[6:]
+    from_left, from_right, window, ranges, cols = rest[6:]
     _, tiles, planes, groups, _ = home_ref.shape
     shift = plan_of(parent_ref, node_count, groups)
     spread_messages(lax.axis_index("node"), from_left, from_right, odd_ref, even_ref, size)
@@ -335,10 +373,13 @@
     for tile in range(tiles):
         for plane in range(planes):
             part = window.at[tile, plane]
-            part[8:16, :] = home_ref[0, tile, plane]
-            part[24:32, :] = home_ref[1, tile, plane]
-            part[32:40, :] = home_ref[3, tile, plane]
-            from_right[tile, plane, 0:8, :] = home_ref[2, tile, plane]
+            home = [home_ref[idx, tile, plane] for idx in range(4)]
+            if tile == tiles - 1 and plane == 0:
+                home = [tail_ref[idx] for idx in range(4)]
+            part[8:16, :] = home[0]
+            part[24:32, :] = home[1]
+            part[32:40, :] = home[3]
+            from_right[tile, plane, 0:8, :] = home[2]
             top = jnp.where(
                 chain < shift[0],
                 from_left[tile, plane, 8:16, :],
@@ -368,11 +409,15 @@
     ranges[...] = jnp.zeros(ranges.shape, jnp.float32)
     range_one = wide_row(ranges, 0, one_ref)
     range_two = wide_row(ranges, 1, two_ref)
-    found = operator_q(point, show, fold, range_one, range_two, block_ref, cols, pay)
-    for idx in range(4):
-        for slot in range(4):
-            value_ref[idx, slot] = found[idx][slot]
-    square_ref[...] = squares(found)
+
+    def put(start, stop, found):
+        for idx in range(4):
+            for slot in range(4):
+                value_ref[idx, slot, :, start:stop] = found[idx][slot]
+
+    square_ref[...] = operator_q(
+        point, show, fold, range_one, range_two, block_ref, cols, put
+    )
 
 
 def rate_of(parts_ref, entry_count):
@@ -385,7 +430,7 @@
     rest = rest[7:]
     if far:
         far_ref, rest = rest[0], rest[1:]
-    square_ref, stage, ranges, cols, pay = rest
+    square_ref, stage, ranges, cols = rest
     _, tiles, planes, groups, _ = own_ref.shape
     rate = rate_of(parts_ref, entry_count)
     raw = [[chain_ref[idx, plane] for plane in range(3)] for idx in range(4)]
@@ -400,13 +445,17 @@
     ranges[...] = jnp.zeros(ranges.shape, jnp.float32)
     range_one = wide_row(ranges, 0, one_ref)
     range_two = wide_row(ranges, 1, two_ref)
-    top_value = [value_ref[0, slot] for slot in range(4)]
-    found = operator_q(point, show, fold, range_one, range_two, block_ref, cols, pay, top_value)
-    square_ref[...] = squares(found)
-    for idx in range(4):
-        for slot in range(4):
-            for tile in range(tiles):
-                own_ref[idx, tile, slot] = found[idx][slot][:, tile * LANES : (tile + 1) * LANES]
+
+    def put(start, stop, found):
+        for idx in range(4):
+            for slot in range(4):
+                for lane in range(start, stop, LANES):
+                    row = found[idx][slot][:, lane - start : lane - start + LANES]
+                    own_ref[idx, lane // LANES, slot] = row
+
+    square_ref[...] = operator_q(
+        point, show, fold, range_one, range_two, block_ref, cols, put, value_ref
+    )
     shift = plan_of(parent_ref, node_count, groups)
     fill_messages(
         lax.axis_index("node"),
@@ -427,49 +476,62 @@
 
 
 def last_kernel(node_count, entry_count, size, far, parent_ref, own_ref, odd_ref, even_ref, *rest):
-    if far:
-        far_ref, rest = rest[0], rest[1:]
+    far_ref, rest = (rest[0], rest[1:]) if far else (None, rest)
     parts_ref, logits_ref, new_ref, half_ref, from_left, from_right, window, lined = rest
     _, tiles, planes, groups, _ = own_ref.shape
     hands = logits_ref.shape[-1]
     shift = plan_of(parent_ref, node_count, groups)
     rate = rate_of(parts_ref, entry_count)
-    spread_messages(lax.axis_index("node"), from_left, from_right, odd_ref, even_ref, size)
+    level = pl.program_id(0)
     group = lax.broadcasted_iota(jnp.int32, (groups, LANES), 0)
-    for tile in range(tiles):
-        start = tile * LANES
-        stop = min(start + LANES, hands)
-        for plane in range(planes):
-            part = window.at[tile, plane]
-            part[0:8, :] = own_ref[1, tile, plane]
-            part[24:32, :] = own_ref[2, tile, plane]
-            part[40:48, :] = own_ref[3, tile, plane]
-            from_right[tile, plane, 0:8, :] = own_ref[0, tile, plane]
-            top = from_right[tile, plane, pl.ds(shift[0], 8), :]
-            mid = jnp.where(
-                group + shift[1] < 8,
-                part[pl.ds(shift[1], 8), :],
-                from_right[tile, plane, pl.ds(shift[0] + shift[1], 8), :],
-            )
-            low = jnp.where(
-                group < shift[2],
-                from_left[tile, plane, 8:16, :],
-                part[pl.ds(24 - shift[2], 8), :],
-            )
-            end = jnp.where(
-                group < shift[3],
-                from_left[tile, plane, pl.ds(8 + shift[2], 8), :],
-                part[pl.ds(40 - jnp.minimum(shift[3], 8), 8), :],
-            )
-            if far:
-                part[56 : 56 + FAR, :] = far_ref[tile, plane * FAR : plane * FAR + FAR, :]
-                end = jnp.where(group < shift[3] - 8, part[56:64, :], end)
-            for idx, row in enumerate((top, mid, low, end)):
-                lined[idx, tile, pl.ds(plane, groups, stride=4), :] = row
-        for idx in range(4):
-            value = lined[idx, tile][:, 0 : stop - start]
-            half_ref[0, idx, :, start:stop] = value
-            new_ref[0, idx, :, start:stop] = logits_ref[0, idx, :, start:stop] + rate * value
+
+    @pl.when(level == 0)
+    def _():
+        spread_messages(lax.axis_index("node"), from_left, from_right, odd_ref, even_ref, size)
+
+    def place_level(idx, found):
+        for tile in range(tiles):
+            start = tile * LANES
+            stop = min(start + LANES, hands)
+            for plane in range(planes):
+                row = found(window.at[tile, plane], tile, plane, own_ref[idx, tile, plane])
+                lined[tile, pl.ds(plane, groups, stride=4), :] = row
+            value = lined[tile][:, 0 : stop - start]
+            half_ref[0, 0, :, start:stop] = value
+            new_ref[0, 0, :, start:stop] = logits_ref[0, 0, :, start:stop] + rate * value
+
+    def top(part, tile, plane, own):
+        from_right[tile, plane, 0:8, :] = own
+        return from_right[tile, plane, pl.ds(shift[0], 8), :]
+
+    def mid(part, tile, plane, own):
+        part[0:8, :] = own
+        return jnp.where(
+            group + shift[1] < 8,
+            part[pl.ds(shift[1], 8), :],
+            from_right[tile, plane, pl.ds(shift[0] + shift[1], 8), :],
+        )
+
+    def low(part, tile, plane, own):
+        part[8:16, :] = own
+        return jnp.where(
+            group < shift[2], from_left[tile, plane, 8:16, :], part[pl.ds(8 - shift[2], 8), :]
+        )
+
+    def end(part, tile, plane, own):
+        part[8:16, :] = own
+        row = jnp.where(
+            group < shift[3],
+            from_left[tile, plane, pl.ds(8 + shift[2], 8), :],
+            part[pl.ds(8 - jnp.minimum(shift[3], 8), 8), :],
+        )
+        if far:
+            part[24 : 24 + FAR, :] = far_ref[tile, plane * FAR : plane * FAR + FAR, :]
+            row = jnp.where(group < shift[3] - 8, part[24:32, :], row)
+        return row
+
+    for idx, found in enumerate((top, mid, low, end)):
+        pl.when(level == idx)(functools.partial(place_level, idx, found))
 
 
 def shared_parts(part):
@@ -481,6 +543,7 @@
 def step_of_class(
     size,
     far,
+    home,
     logits,
     pot_size,
     node_type,
@@ -506,19 +569,15 @@
     def stage(planes, rows=32):
         return pltpu.VMEM((tiles, planes, rows, LANES), f32)
 
-    home, *sent = pl.pallas_call(
+    *sent, tail = pl.pallas_call(
         functools.partial(pack_kernel, node_count, size, far),
-        out_shape=message_shapes(levels, 3, groups, wide, size, far),
-        in_specs=[smem] + [vmem] * 3,
-        scratch_shapes=[
-            pltpu.VMEM((levels, tiles, slots, LANES), f32),
-            pltpu.VMEM((LANES, LANES), f32),
-            pltpu.VMEM((LANES, LANES), f32),
-            stage(3),
-        ],
-        compiler_params=limit(12),
+        out_shape=message_shapes(3, wide, size, far)
+        + [jax.ShapeDtypeStruct((levels, groups, LANES), f32)],
+        in_specs=[smem, smem, smem, vmem],
+        scratch_shapes=[stage(3)],
+        compiler_params=limit(8),
         name="pack",
-    )(parent_slot, logits, pot_size, node_type)
+    )(parent_slot, pot_size, node_type, home)
     got = sent_on(sent[0], sent[1], sent[2:], -2)
     blocks = payoff_blocks(hand_rank, live_mask)
     rows = 7 * slots
@@ -527,7 +586,6 @@
         return [
             pltpu.VMEM((8, wide), f32),
             pltpu.VMEM((count, 2 * wide), jnp.bfloat16),
-            pltpu.VMEM((count, wide), f32),
         ]
 
     def cost(count):
@@ -543,16 +601,18 @@
             jax.ShapeDtypeStruct((levels, 4, groups, wide), f32),
             square_shape,
         ),
-        in_specs=[smem] + [vmem] * (4 + len(got)),
+        in_specs=[smem] + [vmem] * (5 + len(got)),
         scratch_shapes=[stage(3), stage(3), stage(3, 64)] + work(rows),
         compiler_params=limit(32),
         cost_estimate=cost(rows),
         name="first",
-    )(parent_slot, home, *got, range_one, range_two, blocks)
+    )(parent_slot, home, tail, *got, range_one, range_two, blocks)
     parts = shared_parts(part)
     own, *sent, part = pl.pallas_call(
         functools.partial(second_kernel, node_count, entry_count, size, far),
-        out_shape=message_shapes(levels, 4, groups, wide, size, far) + [square_shape],
+        out_shape=[jax.ShapeDtypeStruct((levels, tiles, 4, groups, LANES), f32)]
+        + message_shapes(4, wide, size, far)
+        + [square_shape],
         in_specs=[smem] + [vmem] * 6,
         scratch_shapes=[stage(4)] + work(rows - slots),
         compiler_params=limit(32),
@@ -562,16 +622,14 @@
     got = sent_on(sent[0], sent[1], sent[2:], 2)
     parts = shared_parts(part)
     out_shape = jax.ShapeDtypeStruct(logits.shape, f32)
+    by_level = pl.BlockSpec((1, 1, slots, hands), lambda level: (0, level, 0, 0))
     return pl.pallas_call(
         functools.partial(last_kernel, node_count, entry_count, size, far),
         out_shape=(out_shape, out_shape),
-        in_specs=[smem] + [vmem] * (3 + len(got)),
-        scratch_shapes=[
-            stage(4),
-            stage(4),
-            stage(4, 64),
-            pltpu.VMEM((levels, tiles, slots, LANES), f32),
-        ],
+        grid=(levels,),
+        in_specs=[smem] + [vmem] * (2 + len(got)) + [by_level],
+        out_specs=(by_level, by_level),
+        scratch_shapes=[stage(4), stage(4), stage(4), pltpu.VMEM((tiles, slots, LANES), f32)],
         compiler_params=limit(24),
         name="last",
     )(parent_slot, own, *got, parts, logits)
@@ -583,9 +641,11 @@
     branches = [
         functools.partial(step_of_class, size, size == CLASSES[-1]) for size in CLASSES
     ]
+    home, found = prepared(logits, parent_slot)
     return lax.switch(
-        size_class(parent_slot, logits.shape[2] // 4),
+        found[0],
         branches,
+        home,
         logits,
         pot_size,
         node_type,

time: 52.2 us -> 51.6 us (0.989); the launches traced: 51.9 us -> 50.8 us
  waiting for transfers between devices: 3.16 us -> 1.67 us
  Pallas kernels: 14.8 us -> 16.1 us
  blocking collectives: 23.2 us -> 22.4 us
    ppermute x4, waiting for transfers between devices: 3.16 us -> 1.67 us  [sent_on(): got.append(lax.ppermute(message, 'node', pairs))]
    pallas_call x1, Pallas kernels: 2.14 us -> 3.08 us  [step_of_class(): pl.pallas_call(functools.partial(last_kernel, node_count, entry_count, si...]
    all_to_all x2, blocking collectives: 23.2 us -> 22.4 us  [shared_parts(): return lax.all_to_all(spread, ('node', 'board'), 0, 0, tiled=True)]
  transfers between devices with their start and end apart: 4 -> 4, of which waited for: 2 -> 1; matrix products, arithmetic and copies ran while one was open for 0% -> 0% of each run, Pallas kernels for 5% -> 6%
where the time goes in v1:
time: 51.6 us; the launch traced here: 50.8 us
  blocking collectives  22.4 us (43%)
  Pallas kernels  16.1 us (31%)
  starting transfers between devices  9.07 us (18%)
  waiting for transfers between devices  1.67 us (3%)
  between operations  1.33 us (3%)
    all_to_all x2, blocking collectives, shared_parts(): return lax.all_to_all(spread, ('node', 'board'), 0, 0, tiled=True)  22.4 us
    ppermute x4, starting transfers between devices, sent_on(): got.append(lax.ppermute(message, 'node', pairs))  9.07 us
    pallas_call x1, Pallas kernels, step_of_class(): pl.pallas_call(functools.partial(first_kernel, node_count, size, far), ou...  3.51 us
    pallas_call x1, Pallas kernels, step_of_class(): pl.pallas_call(functools.partial(second_kernel, node_count, entry_count,...  3.39 us
    pallas_call x1, Pallas kernels, step_of_class(): pl.pallas_call(functools.partial(last_kernel, node_count, entry_count, si...  3.08 us
    pallas_call x1, Pallas kernels, payoff_blocks(): pl.pallas_call(functools.partial(payoff_kernel, hands), out_shape=jax.Sha...  2.85 us
    pallas_call x1, Pallas kernels, prepared(): pl.pallas_call(functools.partial(prepare_kernel, lax.axis_size('node')),...  1.69 us
    ppermute x4, waiting for transfers between devices, sent_on(): got.append(lax.ppermute(message, 'node', pairs))  1.67 us
  transfers between devices with their start and end apart: 4, of which 1 were waited for; matrix products, arithmetic and copies ran while one was open for 0% of the time, Pallas kernels for 6%

profile of v1, /device:TPU:0, one launch (start us, length us, event | category | flops | bytes accessed | tf_op | source)
XLA Modules:
  0.0 50.8 jit_solution(1958859163280115638)
XLA Ops:
  0.6 1.7 %prepare.1 = (f32[4,11,3,8,128]{4,3,2,1,0:T(8,128)S(1)}, s32[1]{0:T(128)}) custom-call(s32[4,32]{1,0:T(4,128)} %parent_ref.1, f32[1,4,32,1326]{3,2,1,0:T(8,128)} %logits_ref.1), custom_call_target="tpu_custom_call" | custom-call | tf_op jit(solution)/shard_map/prepare/pallas_call | solution.py:150
  3.0 47.7 %conditional.1 = ((f32[1,4,32,1326]{3,2,1,0:T(8,128)}, f32[1,4,32,1326]{3,2,1,0:T(8,128)})) conditional(s32[]{:T(128)} %bitcast.16, (s32[4,32]{1,0:T(4,128)}, f32[4,32]{1,0:T(4,128)}, s32[4,32]{1,0:T(4,128)}, f32[4,11,3,8,128]{4,3,2,1,0:T(8,128)S(1)}, s32[2,1408]{1,0:T(2,128)}, /*index=5*/s32[1,1326]{1,0:T(1,128)}, ...), branch_computations={%region_0.0_spmd, %region_1.0_spmd, %region_2.0_spmd, %region_3.0_... | conditional | flops 3806330880 | bytes 40526632 | solution.py:645
  3.0 0.0 copy-start.4
  3.0 0.0 copy-start.8
  3.0 0.0 copy-start.12
  3.0 1.6 %pack.4 = (f32[11,16,128]{2,1,0:T(8,128)S(1)}, f32[11,16,128]{2,1,0:T(8,128)S(1)}, f32[4,8,128]{2,1,0:T(8,128)S(1)}) custom-call(s32[4,32]{1,0:T(4,128)} %get-tuple-element.80.parent_ref, f32[4,32]{1,0:T(4,128)} %get-tuple-element.82.pot_ref, s32[4,32]{1,0:T(4,128)} %get-tuple-element.83.kind_ref, f32[4,11,3,8,128]{4,3,2,1,0:T(8,128)S(1)} %get-tuple-element.81.home_ref), custom_call_target="tpu_custom_call" | custom-call | tf_op jit(solution)/shard_map/cond/branch_0_fun/pack/pallas_call | solution.py:572
  4.6 7.0 %collective-permute-start = (f32[11,16,128]{2,1,0:T(8,128)S(1)}, f32[11,16,128]{2,1,0:T(8,128)S(1)}, u32[]{:S(2)}, u32[]{:S(2)}) collective-permute-start(f32[11,16,128]{2,1,0:T(8,128)S(1)} %get-tuple-element.85), channel_id=1, source_target_pairs={{2,4},{4,2},{6,8},{8,6},{10,12},{12,10},{14,16},{16,14},{18,20},{2... | collective-permute-start | bytes 270344 | tf_op jit(solution)/shard_map/cond/branch_0_fun/ppermute | solution.py:231
  11.6 0.0 collective-permute-start.1
  11.6 2.8 %payoff.4.rest_2_.rest_3_ = bf16[2816,1408]{1,0:T(8,128)(2,1)S(1)} custom-call(s32[2,1408]{1,0:T(2,128)} %get-tuple-element.89.cards_ref, s32[1,1326]{1,0:T(1,128)} %get-tuple-element.90.rank_ref, s32[1,1326]{1,0:T(1,128)} %get-tuple-element.91.live_ref), custom_call_target="tpu_custom_call" | custom-call | flops 507510784 | bytes 7929856 | tf_op jit(solution)/shard_map/cond/branch_0_fun/payoff/pallas_call | solution.py:59
  14.5 0.0 collective-permute-done.odd_ref
  14.5 1.7 %collective-permute-done.1.even_ref = f32[11,16,128]{2,1,0:T(8,128)S(1)} collective-permute-done((f32[11,16,128]{2,1,0:T(8,128)S(1)}, f32[11,16,128]{2,1,0:T(8,128)S(1)}, u32[]{:S(2)}, u32[]{:S(2)}) %collective-permute-start.1) | collective-permute-done | bytes 90144 | tf_op jit(solution)/shard_map/cond/branch_0_fun/ppermute | solution.py:231
  16.1 0.0 copy-done.4
  16.1 0.0 copy-done.8
  16.2 0.0 copy-done.12
  16.2 0.0 copy-start
  16.2 3.5 %first.4 = (f32[4,3,8,1408]{3,2,1,0:T(8,128)S(1)}, f32[4,4,8,1408]{3,2,1,0:T(8,128)S(1)}, f32[1,128]{1,0:T(1,128)S(1)}) custom-call(s32[4,32]{1,0:T(4,128)S(1)} %copy-done.4, f32[4,11,3,8,128]{4,3,2,1,0:T(8,128)S(1)} %get-tuple-element.81.home_ref, f32[4,8,128]{2,1,0:T(8,128)S(1)} %get-tuple-element.84.tail_ref, ...), custom_call_target="tpu_custom_call" | custom-call | flops 1776287744 | bytes 11894784 | tf_op jit(solution)/shard_map/cond/branch_0_fun/first/pallas_call | solution.py:597
  19.7 10.9 %all_to_all.48 = f32[32,1,128]{2,1,0:T(1,128)S(1)} all-to-all(f32[32,1,128]{2,1,0:T(1,128)S(1)} %broadcast_in_dim.12), channel_id=1, replica_groups=mesh['node'=16,'board'=2] {'node','board'}, dimensions={0} | all-to-all | bytes 32768 | tf_op jit(solution)/shard_map/cond/branch_0_fun/all_to_all | solution.py:540
  30.6 3.4 %second.4 = (f32[4,11,4,8,128]{4,3,2,1,0:T(8,128)S(1)}, f32[11,24,128]{2,1,0:T(8,128)S(1)}, f32[11,24,128]{2,1,0:T(8,128)S(1)}, f32[1,128]{1,0:T(1,128)S(1)}) custom-call(s32[4,32]{1,0:T(4,128)S(1)} %copy-done.4, f32[4,3,8,1408]{3,2,1,0:T(8,128)S(1)} %get-tuple-element.92.chain_ref, f32[4,4,8,1408]{3,2,1,0:T(8,128)S(1)} %get-tuple-element.93.value_ref, ...), custom_call_target="tpu_custom_call" | custom-call | flops 1522532352 | bytes 11894784 | tf_op jit(solution)/shard_map/cond/branch_0_fun/second/pallas_call | solution.py:611
  34.0 0.6 %collective-permute-start.2 = (f32[11,24,128]{2,1,0:T(8,128)S(1)}, f32[11,24,128]{2,1,0:T(8,128)S(1)}, u32[]{:S(2)}, u32[]{:S(2)}) collective-permute-start(f32[11,24,128]{2,1,0:T(8,128)S(1)} %get-tuple-element.96), channel_id=1, source_target_pairs={{2,4},{4,2},{6,8},{8,6},{10,12},{12,10},{14,16},{16,14},{18,20},{2... | collective-permute-start | bytes 405512 | tf_op jit(solution)/shard_map/cond/branch_0_fun/ppermute | solution.py:231
  34.7 1.5 %collective-permute-start.3 = (f32[11,24,128]{2,1,0:T(8,128)S(1)}, f32[11,24,128]{2,1,0:T(8,128)S(1)}, u32[]{:S(2)}, u32[]{:S(2)}) collective-permute-start(f32[11,24,128]{2,1,0:T(8,128)S(1)} %get-tuple-element.97), channel_id=1, source_target_pairs={{0,2},{2,0},{4,6},{6,4},{8,10},{10,8},{12,14},{14,12},{16,18},{18,... | collective-permute-start | bytes 405512 | tf_op jit(solution)/shard_map/cond/branch_0_fun/ppermute | solution.py:231
  36.1 11.5 %all_to_all.49 = f32[32,1,128]{2,1,0:T(1,128)S(1)} all-to-all(f32[32,1,128]{2,1,0:T(1,128)S(1)} %broadcast_in_dim.13), channel_id=1, replica_groups=mesh['node'=16,'board'=2] {'node','board'}, dimensions={0} | all-to-all | bytes 32768 | tf_op jit(solution)/shard_map/cond/branch_0_fun/all_to_all | solution.py:540
  47.6 0.0 collective-permute-done.2.odd_ref
  47.6 0.0 collective-permute-done.3.even_ref
  47.6 0.0 copy-done
  47.6 3.1 %last.4 = (f32[1,4,32,1326]{3,2,1,0:T(8,128)}, f32[1,4,32,1326]{3,2,1,0:T(8,128)}) custom-call(s32[4,32]{1,0:T(4,128)S(1)} %copy-done.4, f32[4,11,4,8,128]{4,3,2,1,0:T(8,128)S(1)} %get-tuple-element.95.own_ref, f32[11,24,128]{2,1,0:T(8,128)S(1)} %collective-permute-done.2.odd_ref, f32[11,24,128]{2,1,0:T(8,128)S(1)} %collective-permute-done.3.even_ref, ...), custom_call_target="tpu_custom_call" | custom-call | tf_op jit(solution)/shard_map/cond/branch_0_fun/last/pallas_call | solution.py:626
  (2 shorter events, 0.0 us)
Async XLA Ops:
  3.0 13.2 %copy-start.4 = (s32[4,32]{1,0:T(4,128)S(1)}, s32[4,32]{1,0:T(4,128)}, u32[]{:S(2)}) copy-start(s32[4,32]{1,0:T(4,128)} %get-tuple-element.80.parent_ref) | copy-start | bytes 1540 | tf_op jit(solution)/shard_map/cond
  3.0 13.1 %copy-start.8 = (f32[1,1326]{1,0:T(1,128)S(1)}, f32[1,1326]{1,0:T(1,128)}, u32[]{:S(2)}) copy-start(f32[1,1326]{1,0:T(1,128)} %get-tuple-element.87.rest_0_.rest_1_) | copy-start | bytes 15916 | tf_op jit(solution)/shard_map/cond
  3.0 13.1 %copy-start.12 = (f32[1,1326]{1,0:T(1,128)S(1)}, f32[1,1326]{1,0:T(1,128)}, u32[]{:S(2)}) copy-start(f32[1,1326]{1,0:T(1,128)} %get-tuple-element.88.rest_1_.rest_2_) | copy-start | bytes 15916 | tf_op jit(solution)/shard_map/cond
  4.6 9.9 %collective-permute-start = (f32[11,16,128]{2,1,0:T(8,128)S(1)}, f32[11,16,128]{2,1,0:T(8,128)S(1)}, u32[]{:S(2)}, u32[]{:S(2)}) collective-permute-start(f32[11,16,128]{2,1,0:T(8,128)S(1)} %get-tuple-element.85), channel_id=1, source_target_pairs={{2,4},{4,2},{6,8},{8,6},{10,12},{12,10},{14,16},{16,14},{18,20},{2... | collective-permute-start | bytes 270344 | tf_op jit(solution)/shard_map/cond/branch_0_fun/ppermute | solution.py:231
  11.6 4.5 %collective-permute-start.1 = (f32[11,16,128]{2,1,0:T(8,128)S(1)}, f32[11,16,128]{2,1,0:T(8,128)S(1)}, u32[]{:S(2)}, u32[]{:S(2)}) collective-permute-start(f32[11,16,128]{2,1,0:T(8,128)S(1)} %get-tuple-element.86), channel_id=1, source_target_pairs={{0,2},{2,0},{4,6},{6,4},{8,10},{10,8},{12,14},{14,12},{16,18},{18,... | collective-permute-start | bytes 270344 | tf_op jit(solution)/shard_map/cond/branch_0_fun/ppermute | solution.py:231
  16.2 31.5 %copy-start = (f32[1,4,32,1326]{3,2,1,0:T(8,128)S(1)}, f32[1,4,32,1326]{3,2,1,0:T(8,128)}, u32[]{:S(2)}) copy-start(f32[1,4,32,1326]{3,2,1,0:T(8,128)} %get-tuple-element.99.rest_1_) | copy-start | bytes 2036740 | tf_op jit(solution)/shard_map/cond
  34.0 13.6 %collective-permute-start.2 = (f32[11,24,128]{2,1,0:T(8,128)S(1)}, f32[11,24,128]{2,1,0:T(8,128)S(1)}, u32[]{:S(2)}, u32[]{:S(2)}) collective-permute-start(f32[11,24,128]{2,1,0:T(8,128)S(1)} %get-tuple-element.96), channel_id=1, source_target_pairs={{2,4},{4,2},{6,8},{8,6},{10,12},{12,10},{14,16},{16,14},{18,20},{2... | collective-permute-start | bytes 405512 | tf_op jit(solution)/shard_map/cond/branch_0_fun/ppermute | solution.py:231
  34.7 13.0 %collective-permute-start.3 = (f32[11,24,128]{2,1,0:T(8,128)S(1)}, f32[11,24,128]{2,1,0:T(8,128)S(1)}, u32[]{:S(2)}, u32[]{:S(2)}) collective-permute-start(f32[11,24,128]{2,1,0:T(8,128)S(1)} %get-tuple-element.97), channel_id=1, source_target_pairs={{0,2},{2,0},{4,6},{6,4},{8,10},{10,8},{12,14},{14,12},{16,18},{18,... | collective-permute-start | bytes 405512 | tf_op jit(solution)/shard_map/cond/branch_0_fun/ppermute | solution.py:231

commit v2 on v1

--- a/solution.py
+++ b/solution.py
@@ -97,38 +97,59 @@
     return jnp.where(shift[3] > groups, len(CLASSES) - 1, found)
 
 
-def fill_message(stage, message_ref, size, blocks, tail_ref):
+def fill_message(stage, message_ref, size, blocks):
     tiles, planes = stage.shape[:2]
     for tile in range(tiles):
         for plane in range(planes):
             for block_ref, level, start in blocks:
-                if tail_ref is not None and tile == tiles - 1 and plane == 0:
-                    block = tail_ref[level]
-                else:
-                    block = block_ref[level, tile, plane]
-                stage[tile, plane, pl.ds(start, 8), :] = block
+                stage[tile, plane, pl.ds(start, 8), :] = block_ref[level, tile, plane]
             message_ref[tile, plane * size : plane * size + size, :] = stage[
                 tile, plane, 8 : 8 + size, :
             ]
 
 
-def fill_messages(
-    node, stage, message_refs, size, block_ref, to_left, to_right, tail_ref=None
-):
+def fill_messages(node, stage, message_refs, size, block_ref, to_left, to_right):
     even = lax.rem(node, 2) == 0
     for message_ref, on_left in zip(message_refs, (even, jnp.logical_not(even))):
         blocks = [
             (block_ref, jnp.where(on_left, near[0], far[0]), jnp.where(on_left, near[1], far[1]))
             for near, far in zip(to_left, to_right)
         ]
-        fill_message(stage, message_ref, size, blocks, tail_ref)
-
-
-def prepare_kernel(node_count, parent_ref, logits_ref, home_ref, class_ref, raw):
+        fill_message(stage, message_ref, size, blocks)
+
+
+def prepare_kernel(
+    node_count,
+    parent_ref,
+    logits_ref,
+    pot_ref,
+    kind_ref,
+    home_ref,
+    shift_ref,
+    class_ref,
+    raw,
+    flat,
+    turned,
+):
     levels, tiles, planes, groups, _ = home_ref.shape
     slots = 4 * groups
     hands = logits_ref.shape[-1]
-    class_ref[0] = class_of(plan_of(parent_ref, node_count, groups), groups)
+    shift = plan_of(parent_ref, node_count, groups)
+    class_ref[0] = class_of(shift, groups)
+    row_id = lax.broadcasted_iota(jnp.int32, shift_ref.shape, 0)
+    spread = jnp.zeros(shift_ref.shape, jnp.int32)
+    for idx in range(4):
+        spread = jnp.where(row_id == idx, shift[idx], spread)
+    shift_ref[...] = spread
+    pot = pot_ref[...]
+    kind = kind_ref[...]
+    level = lax.broadcasted_iota(jnp.int32, pot.shape, 0)
+    sign = jnp.where(level % 2 == 0, -1.0, 1.0)
+    flat[...] = jnp.zeros(flat.shape, jnp.float32)
+    flat[0:levels, 0:slots] = jnp.where(kind == 2, pot, 0.0)
+    flat[levels : 2 * levels, 0:slots] = jnp.where(kind == 1, pot, 0.0) * sign
+    turned[...] = flat[...].T
+    lane = lax.broadcasted_iota(jnp.int32, (groups, LANES), 1)
     for idx in range(levels):
         raw[idx, tiles - 1] = jnp.zeros((slots, LANES), jnp.float32)
         for tile in range(tiles):
@@ -138,10 +159,16 @@
             first = raw[idx, tile, pl.ds(0, groups, stride=4), :]
             for plane in range(planes):
                 row = raw[idx, tile, pl.ds(plane + 1, groups, stride=4), :] - first
+                if tile == tiles - 1 and plane == 0:
+                    for slot in range(4):
+                        scale = turned[pl.ds(slot, groups, stride=4), :]
+                        row = jnp.where(lane == LANES - 8 + slot, scale[:, idx : idx + 1], row)
+                        fold = scale[:, levels + idx : levels + idx + 1]
+                        row = jnp.where(lane == LANES - 4 + slot, fold, row)
                 home_ref[idx, tile, plane] = row
 
 
-def prepared(logits, parent_slot):
+def prepared(logits, pot_size, node_type, parent_slot):
     _, levels, slots, hands = logits.shape
     groups = slots // 4
     tiles = padded(hands) // LANES
@@ -151,49 +178,30 @@
         functools.partial(prepare_kernel, lax.axis_size("node")),
         out_shape=(
             jax.ShapeDtypeStruct((levels, tiles, 3, groups, LANES), jnp.float32),
+            jax.ShapeDtypeStruct((8, LANES), jnp.int32),
             jax.ShapeDtypeStruct((1,), jnp.int32),
         ),
-        in_specs=[smem, vmem],
-        out_specs=(vmem, smem),
-        scratch_shapes=[pltpu.VMEM((levels, tiles, slots, LANES), jnp.float32)],
+        in_specs=[smem] + [vmem] * 3,
+        out_specs=(vmem, vmem, smem),
+        scratch_shapes=[
+            pltpu.VMEM((levels, tiles, slots, LANES), jnp.float32),
+            pltpu.VMEM((LANES, LANES), jnp.float32),
+            pltpu.VMEM((LANES, LANES), jnp.float32),
+        ],
         compiler_params=pltpu.CompilerParams(vmem_limit_bytes=10 * MEBI),
         name="prepare",
-    )(parent_slot, logits)
-
-
-def pack_kernel(
-    node_count,
-    size,
-    far,
-    parent_ref,
-    pot_ref,
-    kind_ref,
-    home_ref,
-    odd_ref,
-    even_ref,
-    *rest,
-):
+    )(parent_slot, logits, pot_size, node_type)
+
+
+def shifts_in(shift_ref):
+    return [jnp.max(shift_ref[idx : idx + 1, :]) for idx in range(4)]
+
+
+def pack_kernel(size, far, shift_ref, home_ref, _pot, _kind, _parent, odd_ref, even_ref, *rest):
     far_ref = rest[0] if far else None
-    tail_ref, stage = rest[-2:]
-    levels, tiles, planes, groups, _ = home_ref.shape
-    group = lax.broadcasted_iota(jnp.int32, (groups, LANES), 0)
-    lane = lax.broadcasted_iota(jnp.int32, (groups, LANES), 1)
-    spot = [
-        [(group == row) & (lane == LANES - 8 + column) for column in range(8)]
-        for row in range(groups)
-    ]
-    for idx in range(levels):
-        sign = -1.0 if idx % 2 == 0 else 1.0
-        row = home_ref[idx, tiles - 1, 0]
-        for place in range(4 * groups):
-            pot = pot_ref[idx, place]
-            kind = kind_ref[idx, place]
-            show = jnp.where(kind == 2, pot, 0.0)
-            fold = jnp.where(kind == 1, pot, 0.0) * sign
-            row = jnp.where(spot[place // 4][place % 4], show, row)
-            row = jnp.where(spot[place // 4][place % 4 + 4], fold, row)
-        tail_ref[idx] = row
-    shift = plan_of(parent_ref, node_count, groups)
+    stage = rest[-1]
+    _, tiles, planes, groups, _ = home_ref.shape
+    shift = shifts_in(shift_ref)
     fill_messages(
         lax.axis_index("node"),
         stage,
@@ -202,15 +210,11 @@
         home_ref,
         [(2, 8), (3, 8 + shift[2])],
         [(1, shift[0] + shift[1]), (0, shift[0])],
-        tail_ref,
     )
     if far:
         for tile in range(tiles):
             for plane in range(planes):
-                block = home_ref[3, tile, plane]
-                if tile == tiles - 1 and plane == 0:
-                    block = tail_ref[3]
-                far_ref[tile, plane * FAR : plane * FAR + FAR, :] = block[0:FAR, :]
+                far_ref[tile, plane * FAR : plane * FAR + FAR, :] = home_ref[3, tile, plane, 0:FAR, :]
 
 
 def message_shapes(planes, wide, size, far):
@@ -360,13 +364,13 @@
     return store[place : place + 1, :]
 
 
-def first_kernel(node_count, size, far, parent_ref, home_ref, tail_ref, odd_ref, even_ref, *rest):
+def first_kernel(size, far, shift_ref, home_ref, odd_ref, even_ref, *rest):
     if far:
         far_ref, rest = rest[0], rest[1:]
     one_ref, two_ref, block_ref, chain_ref, value_ref, square_ref = rest[:6]
     from_left, from_right, window, ranges, cols = rest[6:]
     _, tiles, planes, groups, _ = home_ref.shape
-    shift = plan_of(parent_ref, node_count, groups)
+    shift = shifts_in(shift_ref)
     spread_messages(lax.axis_index("node"), from_left, from_right, odd_ref, even_ref, size)
     chain = lax.broadcasted_iota(jnp.int32, (groups, LANES), 0)
     point = [[[] for _ in range(planes)] for _ in range(4)]
@@ -374,8 +378,6 @@
         for plane in range(planes):
             part = window.at[tile, plane]
             home = [home_ref[idx, tile, plane] for idx in range(4)]
-            if tile == tiles - 1 and plane == 0:
-                home = [tail_ref[idx] for idx in range(4)]
             part[8:16, :] = home[0]
             part[24:32, :] = home[1]
             part[32:40, :] = home[3]
@@ -425,7 +427,7 @@
     return step_scale / jnp.sqrt(square_sum / entry_count + eps_value)
 
 
-def second_kernel(node_count, entry_count, size, far, parent_ref, chain_ref, value_ref, *rest):
+def second_kernel(entry_count, size, far, shift_ref, chain_ref, value_ref, *rest):
     parts_ref, one_ref, two_ref, block_ref, own_ref, odd_ref, even_ref = rest[:7]
     rest = rest[7:]
     if far:
@@ -456,7 +458,7 @@
     square_ref[...] = operator_q(
         point, show, fold, range_one, range_two, block_ref, cols, put, value_ref
     )
-    shift = plan_of(parent_ref, node_count, groups)
+    shift = shifts_in(shift_ref)
     fill_messages(
         lax.axis_index("node"),
         stage,
@@ -475,30 +477,42 @@
                 far_ref[tile, plane * FAR : plane * FAR + FAR, :] = stage[tile, plane, 8 : 8 + FAR, :]
 
 
-def last_kernel(node_count, entry_count, size, far, parent_ref, own_ref, odd_ref, even_ref, *rest):
+def last_kernel(entry_count, size, far, shift_ref, own_ref, odd_ref, even_ref, *rest):
     far_ref, rest = (rest[0], rest[1:]) if far else (None, rest)
-    parts_ref, logits_ref, new_ref, half_ref, from_left, from_right, window, lined = rest
-    _, tiles, planes, groups, _ = own_ref.shape
+    parts_ref, logits_hbm, new_hbm, half_hbm, from_left, from_right, window, lined = rest[:8]
+    logits_ref, new_ref, half_ref, sems = rest[8:]
+    levels, tiles, planes, groups, _ = own_ref.shape
     hands = logits_ref.shape[-1]
-    shift = plan_of(parent_ref, node_count, groups)
+    fetches = [
+        pltpu.make_async_copy(logits_hbm.at[0, idx], logits_ref.at[idx], sems.at[0, idx])
+        for idx in range(levels)
+    ]
+    for fetch in fetches:
+        fetch.start()
+    shift = shifts_in(shift_ref)
     rate = rate_of(parts_ref, entry_count)
-    level = pl.program_id(0)
     group = lax.broadcasted_iota(jnp.int32, (groups, LANES), 0)
-
-    @pl.when(level == 0)
-    def _():
-        spread_messages(lax.axis_index("node"), from_left, from_right, odd_ref, even_ref, size)
+    spread_messages(lax.axis_index("node"), from_left, from_right, odd_ref, even_ref, size)
+    leaving = []
 
     def place_level(idx, found):
         for tile in range(tiles):
+            for plane in range(planes):
+                row = found(window.at[tile, plane], tile, plane, own_ref[idx, tile, plane])
+                lined[idx, tile, pl.ds(plane, groups, stride=4), :] = row
             start = tile * LANES
             stop = min(start + LANES, hands)
-            for plane in range(planes):
-                row = found(window.at[tile, plane], tile, plane, own_ref[idx, tile, plane])
-                lined[tile, pl.ds(plane, groups, stride=4), :] = row
-            value = lined[tile][:, 0 : stop - start]
-            half_ref[0, 0, :, start:stop] = value
-            new_ref[0, 0, :, start:stop] = logits_ref[0, 0, :, start:stop] + rate * value
+            half_ref[idx, :, start:stop] = lined[idx, tile][:, 0 : stop - start]
+        leaving.append(
+            pltpu.make_async_copy(half_ref.at[idx], half_hbm.at[0, idx], sems.at[1, idx])
+        )
+        leaving[-1].start()
+        fetches[idx].wait()
+        new_ref[idx] = logits_ref[idx] + rate * half_ref[idx]
+        leaving.append(
+            pltpu.make_async_copy(new_ref.at[idx], new_hbm.at[0, idx], sems.at[2, idx])
+        )
+        leaving[-1].start()
 
     def top(part, tile, plane, own):
         from_right[tile, plane, 0:8, :] = own
@@ -531,7 +545,9 @@
         return row
 
     for idx, found in enumerate((top, mid, low, end)):
-        pl.when(level == idx)(functools.partial(place_level, idx, found))
+        place_level(idx, found)
+    for copy in leaving:
+        copy.wait()
 
 
 def shared_parts(part):
@@ -544,6 +560,7 @@
     size,
     far,
     home,
+    shift,
     logits,
     pot_size,
     node_type,
@@ -557,10 +574,8 @@
     wide = padded(hands)
     tiles = wide // LANES
     groups = slots // 4
-    node_count = lax.axis_size("node")
-    entry_count = float(logits.size * node_count * lax.axis_size("board"))
+    entry_count = float(logits.size * lax.axis_size("node") * lax.axis_size("board"))
     vmem = pl.BlockSpec(memory_space=pltpu.VMEM)
-    smem = pl.BlockSpec(memory_space=pltpu.SMEM)
     f32 = jnp.float32
 
     def limit(mebi):
@@ -569,15 +584,15 @@
     def stage(planes, rows=32):
         return pltpu.VMEM((tiles, planes, rows, LANES), f32)
 
-    *sent, tail = pl.pallas_call(
-        functools.partial(pack_kernel, node_count, size, far),
-        out_shape=message_shapes(3, wide, size, far)
-        + [jax.ShapeDtypeStruct((levels, groups, LANES), f32)],
-        in_specs=[smem, smem, smem, vmem],
+    anywhere = pl.BlockSpec(memory_space=pl.ANY)
+    sent = pl.pallas_call(
+        functools.partial(pack_kernel, size, far),
+        out_shape=message_shapes(3, wide, size, far),
+        in_specs=[vmem, vmem] + [anywhere] * 3,
         scratch_shapes=[stage(3)],
         compiler_params=limit(8),
         name="pack",
-    )(parent_slot, pot_size, node_type, home)
+    )(shift, home, pot_size, node_type, parent_slot)
     got = sent_on(sent[0], sent[1], sent[2:], -2)
     blocks = payoff_blocks(hand_rank, live_mask)
     rows = 7 * slots
@@ -595,44 +610,52 @@
 
     square_shape = jax.ShapeDtypeStruct((1, LANES), f32)
     chain, value, part = pl.pallas_call(
-        functools.partial(first_kernel, node_count, size, far),
+        functools.partial(first_kernel, size, far),
         out_shape=(
             jax.ShapeDtypeStruct((levels, 3, groups, wide), f32),
             jax.ShapeDtypeStruct((levels, 4, groups, wide), f32),
             square_shape,
         ),
-        in_specs=[smem] + [vmem] * (5 + len(got)),
+        in_specs=[vmem] * (5 + len(got)),
         scratch_shapes=[stage(3), stage(3), stage(3, 64)] + work(rows),
         compiler_params=limit(32),
         cost_estimate=cost(rows),
         name="first",
-    )(parent_slot, home, tail, *got, range_one, range_two, blocks)
+    )(shift, home, *got, range_one, range_two, blocks)
     parts = shared_parts(part)
     own, *sent, part = pl.pallas_call(
-        functools.partial(second_kernel, node_count, entry_count, size, far),
+        functools.partial(second_kernel, entry_count, size, far),
         out_shape=[jax.ShapeDtypeStruct((levels, tiles, 4, groups, LANES), f32)]
         + message_shapes(4, wide, size, far)
         + [square_shape],
-        in_specs=[smem] + [vmem] * 6,
+        in_specs=[vmem] * 7,
         scratch_shapes=[stage(4)] + work(rows - slots),
         compiler_params=limit(32),
         cost_estimate=cost(rows - slots),
         name="second",
-    )(parent_slot, chain, value, parts, range_one, range_two, blocks)
+    )(shift, chain, value, parts, range_one, range_two, blocks)
     got = sent_on(sent[0], sent[1], sent[2:], 2)
     parts = shared_parts(part)
     out_shape = jax.ShapeDtypeStruct(logits.shape, f32)
-    by_level = pl.BlockSpec((1, 1, slots, hands), lambda level: (0, level, 0, 0))
+    level_shape = (levels, slots, hands)
     return pl.pallas_call(
-        functools.partial(last_kernel, node_count, entry_count, size, far),
+        functools.partial(last_kernel, entry_count, size, far),
         out_shape=(out_shape, out_shape),
-        grid=(levels,),
-        in_specs=[smem] + [vmem] * (2 + len(got)) + [by_level],
-        out_specs=(by_level, by_level),
-        scratch_shapes=[stage(4), stage(4), stage(4), pltpu.VMEM((tiles, slots, LANES), f32)],
+        in_specs=[vmem] * (3 + len(got)) + [anywhere],
+        out_specs=(anywhere, anywhere),
+        scratch_shapes=[
+            stage(4),
+            stage(4),
+            stage(4),
+            pltpu.VMEM((levels, tiles, slots, LANES), f32),
+            pltpu.VMEM(level_shape, f32),
+            pltpu.VMEM(level_shape, f32),
+            pltpu.VMEM(level_shape, f32),
+            pltpu.SemaphoreType.DMA((3, levels)),
+        ],
         compiler_params=limit(24),
         name="last",
-    )(parent_slot, own, *got, parts, logits)
+    )(shift, own, *got, parts, logits)
 
 
 def per_device(
@@ -641,11 +664,12 @@
     branches = [
         functools.partial(step_of_class, size, size == CLASSES[-1]) for size in CLASSES
     ]
-    home, found = prepared(logits, parent_slot)
+    home, shift, found = prepared(logits, pot_size, node_type, parent_slot)
     return lax.switch(
         found[0],
         branches,
         home,
+        shift,
         logits,
         pot_size,
         node_type,

time: 51.6 us -> 50.4 us (0.977)
  Pallas kernels: 16.1 us -> 14.3 us
  loops' own time: 0.1 us -> 0.62 us
    pallas_call x4, Pallas kernels: 11.6 us -> 9.79 us  [the longest x1 3.09 us: step_of_class(): pl.pallas_call(functools.partial(last_kernel, entry_count, size, far), ou...]
where the time goes in v2:
time: 50.4 us; the launch traced here: 49.6 us
  blocking collectives  22.4 us (44%)
  Pallas kernels  14.3 us (28%)
  starting transfers between devices  9.04 us (18%)
  waiting for transfers between devices  1.67 us (3%)
  between operations  1.51 us (3%)
  loops' own time  0.62 us (1%)
    all_to_all x2, blocking collectives, shared_parts(): return lax.all_to_all(spread, ('node', 'board'), 0, 0, tiled=True)  22.4 us
    ppermute x4, starting transfers between devices, sent_on(): got.append(lax.ppermute(message, 'node', pairs))  9.04 us
    pallas_call x1, Pallas kernels, step_of_class(): pl.pallas_call(functools.partial(last_kernel, entry_count, size, far), ou...  3.09 us
    pallas_call x1, Pallas kernels, step_of_class(): pl.pallas_call(functools.partial(second_kernel, entry_count, size, far),...  3.04 us
    pallas_call x1, Pallas kernels, step_of_class(): pl.pallas_call(functools.partial(first_kernel, size, far), out_shape=(jax...  3.03 us
    pallas_call x1, Pallas kernels, payoff_blocks(): pl.pallas_call(functools.partial(payoff_kernel, hands), out_shape=jax.Sha...  2.84 us
    pallas_call x1, Pallas kernels, prepared(): pl.pallas_call(functools.partial(prepare_kernel, lax.axis_size('node')),...  1.7 us
    ppermute x4, waiting for transfers between devices, sent_on(): got.append(lax.ppermute(message, 'node', pairs))  1.67 us
  transfers between devices with their start and end apart: 4, of which 1 were waited for; matrix products, arithmetic and copies ran while one was open for 0% of the time, Pallas kernels for 6%

profile of v2, /device:TPU:0, one launch (start us, length us, event | category | flops | bytes accessed | tf_op | source)
XLA Modules:
  0.0 49.6 jit_solution(6828038289858675571)
XLA Ops:
  0.6 1.7 %prepare.1 = (f32[4,11,3,8,128]{4,3,2,1,0:T(8,128)S(1)}, s32[8,128]{1,0:T(8,128)S(1)}, s32[1]{0:T(128)}) custom-call(s32[4,32]{1,0:T(4,128)} %parent_ref.1, f32[1,4,32,1326]{3,2,1,0:T(8,128)} %logits_ref.1, f32[4,32]{1,0:T(4,128)} %pot_ref.1, s32[4,32]{1,0:T(4,128)} %kind_ref.1), custom_call_target="tpu_custom_call" | custom-call | tf_op jit(solution)/shard_map/prepare/pallas_call | solution.py:177
  3.0 46.4 %conditional.1 = ((f32[1,4,32,1326]{3,2,1,0:T(8,128)}, f32[1,4,32,1326]{3,2,1,0:T(8,128)})) conditional(s32[]{:T(128)} %bitcast.16, (s32[8,128]{1,0:T(8,128)S(1)}, f32[4,11,3,8,128]{4,3,2,1,0:T(8,128)S(1)}, f32[4,32]{1,0:T(4,128)}, s32[4,32]{1,0:T(4,128)}, s32[4,32]{1,0:T(4,128)}, /*index=5*/s32[2,1408]{1,0:T(2,128)}, ...), branch_computations={%region_0.0_spmd, %region_1.0_spmd, %region_2.0_spmd, %region_3.0_... | conditional | flops 3806330880 | bytes 40524556 | solution.py:668
  3.0 0.0 copy-start.4
  3.0 0.0 copy-start.8
  3.0 0.6 %pack.4 = (f32[11,16,128]{2,1,0:T(8,128)S(1)}, f32[11,16,128]{2,1,0:T(8,128)S(1)}) custom-call(s32[8,128]{1,0:T(8,128)S(1)} %get-tuple-element.88.shift_ref, f32[4,11,3,8,128]{4,3,2,1,0:T(8,128)S(1)} %get-tuple-element.89.home_ref, f32[4,32]{1,0:T(4,128)} %get-tuple-element.90._pot, s32[4,32]{1,0:T(4,128)} %get-tuple-element.91._kind, ...), custom_call_target="tpu_custom_call" | custom-call | tf_op jit(solution)/shard_map/cond/branch_0_fun/pack/pallas_call | solution.py:588
  3.7 7.0 %collective-permute-start = (f32[11,16,128]{2,1,0:T(8,128)S(1)}, f32[11,16,128]{2,1,0:T(8,128)S(1)}, u32[]{:S(2)}, u32[]{:S(2)}) collective-permute-start(f32[11,16,128]{2,1,0:T(8,128)S(1)} %get-tuple-element.93), channel_id=1, source_target_pairs={{2,4},{4,2},{6,8},{8,6},{10,12},{12,10},{14,16},{16,14},{18,20},{2... | collective-permute-start | bytes 270344 | tf_op jit(solution)/shard_map/cond/branch_0_fun/ppermute | solution.py:235
  10.6 0.0 collective-permute-start.1
  10.6 2.8 %payoff.4.rest_2_.rest_3_ = bf16[2816,1408]{1,0:T(8,128)(2,1)S(1)} custom-call(s32[2,1408]{1,0:T(2,128)} %get-tuple-element.97.cards_ref, s32[1,1326]{1,0:T(1,128)} %get-tuple-element.98.rank_ref, s32[1,1326]{1,0:T(1,128)} %get-tuple-element.99.live_ref), custom_call_target="tpu_custom_call" | custom-call | flops 507510784 | bytes 7929856 | tf_op jit(solution)/shard_map/cond/branch_0_fun/payoff/pallas_call | solution.py:59
  13.5 0.0 collective-permute-done.odd_ref
  13.5 1.7 %collective-permute-done.1.even_ref = f32[11,16,128]{2,1,0:T(8,128)S(1)} collective-permute-done((f32[11,16,128]{2,1,0:T(8,128)S(1)}, f32[11,16,128]{2,1,0:T(8,128)S(1)}, u32[]{:S(2)}, u32[]{:S(2)}) %collective-permute-start.1) | collective-permute-done | bytes 90144 | tf_op jit(solution)/shard_map/cond/branch_0_fun/ppermute | solution.py:235
  15.2 0.0 copy-done.4
  15.2 0.0 copy-done.8
  15.2 0.0 copy-start
  15.2 3.0 %first.4 = (f32[4,3,8,1408]{3,2,1,0:T(8,128)S(1)}, f32[4,4,8,1408]{3,2,1,0:T(8,128)S(1)}, f32[1,128]{1,0:T(1,128)S(1)}) custom-call(s32[8,128]{1,0:T(8,128)S(1)} %get-tuple-element.88.shift_ref, f32[4,11,3,8,128]{4,3,2,1,0:T(8,128)S(1)} %get-tuple-element.89.home_ref, f32[11,16,128]{2,1,0:T(8,128)S(1)} %collective-permute-done.odd_ref, ...), custom_call_target="tpu_custom_call" | custom-call | flops 1776287744 | bytes 11894784 | tf_op jit(solution)/shard_map/cond/branch_0_fun/first/pallas_call | solution.py:612
  18.2 10.9 %all_to_all.48 = f32[32,1,128]{2,1,0:T(1,128)S(1)} all-to-all(f32[32,1,128]{2,1,0:T(1,128)S(1)} %broadcast_in_dim.12), channel_id=1, replica_groups=mesh['node'=16,'board'=2] {'node','board'}, dimensions={0} | all-to-all | bytes 32768 | tf_op jit(solution)/shard_map/cond/branch_0_fun/all_to_all | solution.py:556
  29.2 3.0 %second.4 = (f32[4,11,4,8,128]{4,3,2,1,0:T(8,128)S(1)}, f32[11,24,128]{2,1,0:T(8,128)S(1)}, f32[11,24,128]{2,1,0:T(8,128)S(1)}, f32[1,128]{1,0:T(1,128)S(1)}) custom-call(s32[8,128]{1,0:T(8,128)S(1)} %get-tuple-element.88.shift_ref, f32[4,3,8,1408]{3,2,1,0:T(8,128)S(1)} %get-tuple-element.100.chain_ref, f32[4,4,8,1408]{3,2,1,0:T(8,128)S(1)} %get-tuple-element.101.value_ref, ...), custom_call_target="tpu_custom_call" | custom-call | flops 1522532352 | bytes 11894784 | tf_op jit(solution)/shard_map/cond/branch_0_fun/second/pallas_call | solution.py:626
  32.2 0.6 %collective-permute-start.2 = (f32[11,24,128]{2,1,0:T(8,128)S(1)}, f32[11,24,128]{2,1,0:T(8,128)S(1)}, u32[]{:S(2)}, u32[]{:S(2)}) collective-permute-start(f32[11,24,128]{2,1,0:T(8,128)S(1)} %get-tuple-element.104), channel_id=1, source_target_pairs={{2,4},{4,2},{6,8},{8,6},{10,12},{12,10},{14,16},{16,14},{18,20},{2... | collective-permute-start | bytes 405512 | tf_op jit(solution)/shard_map/cond/branch_0_fun/ppermute | solution.py:235
  32.8 1.4 %collective-permute-start.3 = (f32[11,24,128]{2,1,0:T(8,128)S(1)}, f32[11,24,128]{2,1,0:T(8,128)S(1)}, u32[]{:S(2)}, u32[]{:S(2)}) collective-permute-start(f32[11,24,128]{2,1,0:T(8,128)S(1)} %get-tuple-element.105), channel_id=1, source_target_pairs={{0,2},{2,0},{4,6},{6,4},{8,10},{10,8},{12,14},{14,12},{16,18},{18,... | collective-permute-start | bytes 405512 | tf_op jit(solution)/shard_map/cond/branch_0_fun/ppermute | solution.py:235
  34.3 11.5 %all_to_all.49 = f32[32,1,128]{2,1,0:T(1,128)S(1)} all-to-all(f32[32,1,128]{2,1,0:T(1,128)S(1)} %broadcast_in_dim.13), channel_id=1, replica_groups=mesh['node'=16,'board'=2] {'node','board'}, dimensions={0} | all-to-all | bytes 32768 | tf_op jit(solution)/shard_map/cond/branch_0_fun/all_to_all | solution.py:556
  45.8 0.0 collective-permute-done.2.odd_ref
  45.8 0.0 collective-permute-done.3.even_ref
  45.8 0.0 copy-done
  45.8 3.1 %last.4 = (f32[1,4,32,1326]{3,2,1,0:T(8,128)}, f32[1,4,32,1326]{3,2,1,0:T(8,128)}) custom-call(s32[8,128]{1,0:T(8,128)S(1)} %get-tuple-element.88.shift_ref, f32[4,11,4,8,128]{4,3,2,1,0:T(8,128)S(1)} %get-tuple-element.103.own_ref, f32[11,24,128]{2,1,0:T(8,128)S(1)} %collective-permute-done.2.odd_ref, f32[11,24,128]{2,1,0:T(8,128)S(1)} %collective-permute-done.3.even_ref, ...), custom_call_target="tpu_custom_call" | custom-call | tf_op jit(solution)/shard_map/cond/branch_0_fun/last/pallas_call | solution.py:641
  (2 shorter events, 0.0 us)
Async XLA Ops:
  3.0 12.2 %copy-start.4 = (f32[1,1326]{1,0:T(1,128)S(1)}, f32[1,1326]{1,0:T(1,128)}, u32[]{:S(2)}) copy-start(f32[1,1326]{1,0:T(1,128)} %get-tuple-element.95.rest_0_.rest_1_) | copy-start | bytes 15916 | tf_op jit(solution)/shard_map/cond
  3.0 12.2 %copy-start.8 = (f32[1,1326]{1,0:T(1,128)S(1)}, f32[1,1326]{1,0:T(1,128)}, u32[]{:S(2)}) copy-start(f32[1,1326]{1,0:T(1,128)} %get-tuple-element.96.rest_1_.rest_2_) | copy-start | bytes 15916 | tf_op jit(solution)/shard_map/cond
  3.7 9.8 %collective-permute-start = (f32[11,16,128]{2,1,0:T(8,128)S(1)}, f32[11,16,128]{2,1,0:T(8,128)S(1)}, u32[]{:S(2)}, u32[]{:S(2)}) collective-permute-start(f32[11,16,128]{2,1,0:T(8,128)S(1)} %get-tuple-element.93), channel_id=1, source_target_pairs={{2,4},{4,2},{6,8},{8,6},{10,12},{12,10},{14,16},{16,14},{18,20},{2... | collective-permute-start | bytes 270344 | tf_op jit(solution)/shard_map/cond/branch_0_fun/ppermute | solution.py:235
  10.6 4.5 %collective-permute-start.1 = (f32[11,16,128]{2,1,0:T(8,128)S(1)}, f32[11,16,128]{2,1,0:T(8,128)S(1)}, u32[]{:S(2)}, u32[]{:S(2)}) collective-permute-start(f32[11,16,128]{2,1,0:T(8,128)S(1)} %get-tuple-element.94), channel_id=1, source_target_pairs={{0,2},{2,0},{4,6},{6,4},{8,10},{10,8},{12,14},{14,12},{16,18},{18,... | collective-permute-start | bytes 270344 | tf_op jit(solution)/shard_map/cond/branch_0_fun/ppermute | solution.py:235
  15.2 30.6 %copy-start = (f32[1,4,32,1326]{3,2,1,0:T(8,128)S(1)}, f32[1,4,32,1326]{3,2,1,0:T(8,128)}, u32[]{:S(2)}) copy-start(f32[1,4,32,1326]{3,2,1,0:T(8,128)} %get-tuple-element.107.rest_1_) | copy-start | bytes 2036740 | tf_op jit(solution)/shard_map/cond
  32.2 13.6 %collective-permute-start.2 = (f32[11,24,128]{2,1,0:T(8,128)S(1)}, f32[11,24,128]{2,1,0:T(8,128)S(1)}, u32[]{:S(2)}, u32[]{:S(2)}) collective-permute-start(f32[11,24,128]{2,1,0:T(8,128)S(1)} %get-tuple-element.104), channel_id=1, source_target_pairs={{2,4},{4,2},{6,8},{8,6},{10,12},{12,10},{14,16},{16,14},{18,20},{2... | collective-permute-start | bytes 405512 | tf_op jit(solution)/shard_map/cond/branch_0_fun/ppermute | solution.py:235
  32.8 13.0 %collective-permute-start.3 = (f32[11,24,128]{2,1,0:T(8,128)S(1)}, f32[11,24,128]{2,1,0:T(8,128)S(1)}, u32[]{:S(2)}, u32[]{:S(2)}) collective-permute-start(f32[11,24,128]{2,1,0:T(8,128)S(1)} %get-tuple-element.105), channel_id=1, source_target_pairs={{0,2},{2,0},{4,6},{6,4},{8,10},{10,8},{12,14},{14,12},{16,18},{18,... | collective-permute-start | bytes 405512 | tf_op jit(solution)/shard_map/cond/branch_0_fun/ppermute | solution.py:235
